TPU v7x, 32 devices: a whole 2x2x4 slice. The times are simulated.
32 devices in a mesh: layer: 4 (over y, core), unit: 8 (over z, x).
Axes of the slice: x: 2, y: 2, z: 4, core: 2. Of those that a mesh axis runs over, the one named last changes fastest.
Arguments:
- tokens: int32 [4, 32], replicated, may hold values from 0 to 255
- embed: bfloat16 [256, 8192], P(None, 'unit'), may hold values from -6 to 6
- weights: bfloat16 [4, 128, 32, 64, 256], P('layer', 'unit'), may hold values from -0.125 to 0.125
- layout: int32 [4, 128, 32], P('layer', 'unit'), may hold values from 0 to 255, as said below
- bias: float32 [4, 128, 256], P('layer', 'unit'), may hold values from -4 to 4
- d_hidden: bfloat16 [4, 4, 32, 8192], P('layer', None, None, 'unit'), may hold values from -6 to 6
Outputs:
- hidden: bfloat16 [4, 4, 32, 8192], P('layer', None, None, 'unit')
- grad_weights: bfloat16 [4, 128, 32, 64, 256], P('layer', 'unit')
- grad_bias: float32 [4, 128, 256], P('layer', 'unit')
Inputs may be any that keep to these rules, and one draw needn't show every extreme that they name: The 32 entries of every row layout[l, j] are distinct and rising; numbers under 128 are blocks of the layer's input, the others of its own previous hidden state.
All inputs are finite; a program needn't handle non-finite values.
Results may differ from a plain program's by a relative error of at most 0.0085.
Values may be sent and summed in bfloat16 or wider, within the bound.
A program may use at most 128 MiB of HBM per device.

v0:
```python
import jax
import jax.numpy as jnp
from jax import lax
from jax.sharding import PartitionSpec as P


def passed_along(value, axis, steps):
    count = lax.axis_size(axis)
    leading, last = (max(0, -steps), min(count, count - steps))
    return lax.ppermute(value, axis, [(source, source + steps) for source in range(leading, last)])


def gate_math(pre_act, cell_prev):
    gate_size = pre_act.shape[-1] // 4
    in_gate = jax.nn.sigmoid(pre_act[..., :gate_size])
    forget = jax.nn.sigmoid(pre_act[..., gate_size : 2 * gate_size])
    update = jnp.tanh(pre_act[..., 2 * gate_size : 3 * gate_size])
    out_gate = jax.nn.sigmoid(pre_act[..., 3 * gate_size :])
    cell_state = forget * cell_prev + in_gate * update
    new_hidden = (out_gate * jnp.tanh(cell_state)).astype(jnp.bfloat16)
    return (jnp.concatenate([in_gate, forget, update, out_gate], -1), cell_state, new_hidden)


def gate_grads(gate_acts, cell_state, cell_prev, grad_hidden, grad_carry):
    gate_size = gate_acts.shape[-1] // 4
    in_gate = gate_acts[..., :gate_size]
    forget = gate_acts[..., gate_size : 2 * gate_size]
    update = gate_acts[..., 2 * gate_size : 3 * gate_size]
    out_gate = gate_acts[..., 3 * gate_size :]
    squash = jnp.tanh(cell_state)
    grad_cell = grad_carry + grad_hidden * out_gate * (1.0 - squash * squash)
    grad_in = grad_cell * update * in_gate * (1.0 - in_gate)
    grad_forget = grad_cell * cell_prev * forget * (1.0 - forget)
    grad_update = grad_cell * in_gate * (1.0 - update * update)
    grad_out = grad_hidden * squash * out_gate * (1.0 - out_gate)
    grad_pre = jnp.concatenate([grad_in, grad_forget, grad_update, grad_out], -1).astype(
        jnp.bfloat16
    )
    return (grad_pre, grad_cell * forget)


def to_blocks(rows_arr):
    return rows_arr.transpose(1, 0, 2).reshape(
        rows_arr.shape[1], rows_arr.shape[0] * rows_arr.shape[2]
    )


def from_blocks(block_arr, batch_rows, block_size):
    return block_arr.reshape(block_arr.shape[0], batch_rows, block_size).transpose(1, 0, 2)


def on_device(tokens, embed, weights, layout, bias, d_hidden):
    layer_count = lax.axis_size("layer")
    layer_idx = lax.axis_index("layer")
    unit_count = lax.axis_size("unit")
    step_count, batch_rows = tokens.shape
    vocab_size, unit_width = embed.shape
    weight_blocks = weights[0]
    layout_rows = layout[0]
    bias_rows = bias[0]
    cotangent = d_hidden[0]
    own_blocks, nonzero, block_size, gate_width = weight_blocks.shape
    full_width = unit_width * unit_count
    all_blocks = full_width // block_size
    wave_count = step_count + layer_count - 1
    row_width = batch_rows * block_size
    vocab_ids = jnp.arange(vocab_size, dtype=jnp.int32)
    flat_layout = layout_rows.reshape(-1)
    full_table = lax.all_gather(embed, "unit", axis=1, tiled=True).reshape(
        vocab_size, all_blocks, block_size
    )

    def lookup(time_step, table3):
        ids_row = lax.dynamic_index_in_dim(tokens, time_step, 0, False)
        onehot = (ids_row[:, None] == vocab_ids[None, :]).astype(jnp.bfloat16)
        looked = jnp.einsum("bv,vjc->jbc", onehot, table3, preferred_element_type=jnp.float32)
        return looked.astype(jnp.bfloat16).reshape(table3.shape[1], row_width)

    def forward_wave(wave_idx, loop_state):
        hidden_own, cell_state, stored, cell_log, act_log, hidden_log = loop_state
        time_step = wave_idx - layer_idx
        in_range = (time_step >= 0) & (time_step < step_count)
        clipped = jnp.clip(time_step, 0, step_count - 1)
        slot = jnp.where(in_range, time_step, step_count)
        hidden_full = lax.all_gather(hidden_own, "unit", axis=0, tiled=True)
        below_full = passed_along(hidden_full, "layer", 1)
        source_full = jnp.where(layer_idx == 0, lookup(clipped, full_table), below_full)
        inputs = jnp.concatenate([source_full, hidden_full], 0)
        picked = jnp.take(inputs, flat_layout, axis=0).reshape(
            own_blocks, nonzero, batch_rows, block_size
        )
        pre_act = (
            jnp.einsum("jkbc,jkcd->bjd", picked, weight_blocks, preferred_element_type=jnp.float32)
            + bias_rows
        )
        gate_acts, new_cell, new_hidden = gate_math(pre_act, cell_state)
        hidden_own = jnp.where(in_range, to_blocks(new_hidden), hidden_own)
        cell_state = jnp.where(in_range, new_cell, cell_state)
        stored = lax.dynamic_update_index_in_dim(stored, inputs, slot, 0)
        cell_log = lax.dynamic_update_index_in_dim(cell_log, new_cell, slot, 0)
        act_log = lax.dynamic_update_index_in_dim(act_log, gate_acts, slot, 0)
        hidden_log = lax.dynamic_update_index_in_dim(
            hidden_log, new_hidden.reshape(batch_rows, unit_width), slot, 0
        )
        return (hidden_own, cell_state, stored, cell_log, act_log, hidden_log)

    start = (
        jnp.zeros((own_blocks, row_width), jnp.bfloat16),
        jnp.zeros((batch_rows, own_blocks, block_size), jnp.float32),
        jnp.zeros((step_count + 1, 2 * all_blocks, row_width), jnp.bfloat16),
        jnp.zeros((step_count + 1, batch_rows, own_blocks, block_size), jnp.float32),
        jnp.zeros((step_count + 1, batch_rows, own_blocks, gate_width), jnp.float32),
        jnp.zeros((step_count + 1, batch_rows, unit_width), jnp.bfloat16),
    )
    _, _, stored, cell_log, act_log, hidden_log = lax.fori_loop(0, wave_count, forward_wave, start)

    def backward_wave(wave_idx, loop_state):
        send_down, grad_recur, grad_carry, pre_log = loop_state
        time_step = step_count - 1 - wave_idx + (layer_count - 1 - layer_idx)
        in_range = (time_step >= 0) & (time_step < step_count)
        clipped = jnp.clip(time_step, 0, step_count - 1)
        slot = jnp.where(in_range, time_step, step_count)
        from_above = passed_along(send_down.astype(jnp.bfloat16), "layer", -1).astype(
            send_down.dtype
        )
        upstream = lax.dynamic_index_in_dim(cotangent, clipped, 0, False).astype(jnp.float32)
        grad_hidden = (
            upstream.reshape(batch_rows, own_blocks, block_size)
            + from_blocks(from_above, batch_rows, block_size)
            + grad_recur
        )
        gate_acts = lax.dynamic_index_in_dim(act_log, clipped, 0, False)
        cell_state = lax.dynamic_index_in_dim(cell_log, clipped, 0, False)
        prev_index = jnp.maximum(clipped - 1, 0)
        cell_prev = lax.dynamic_index_in_dim(cell_log, prev_index, 0, False) * (clipped > 0).astype(
            jnp.float32
        )
        grad_pre, carry_new = gate_grads(gate_acts, cell_state, cell_prev, grad_hidden, grad_carry)
        contrib = jnp.einsum(
            "bjd,jkcd->jkbc", grad_pre, weight_blocks, preferred_element_type=jnp.float32
        )
        partial_value = (
            jnp.zeros((2 * all_blocks, row_width), jnp.float32)
            .at[flat_layout]
            .add(contrib.reshape(own_blocks * nonzero, row_width))
        )
        halves = partial_value.reshape(2, all_blocks, row_width)
        summed = lax.psum_scatter(
            halves.astype(jnp.bfloat16), "unit", scatter_dimension=1, tiled=True
        ).astype(jnp.float32)
        source_sum = summed[0]
        recur_sum = summed[1]
        send_down = jnp.where(in_range, source_sum, jnp.zeros_like(send_down))
        grad_recur = jnp.where(in_range, from_blocks(recur_sum, batch_rows, block_size), grad_recur)
        grad_carry = jnp.where(in_range, carry_new, grad_carry)
        pre_log = lax.dynamic_update_index_in_dim(pre_log, grad_pre, slot, 0)
        return (send_down, grad_recur, grad_carry, pre_log)

    start = (
        jnp.zeros((own_blocks, row_width), jnp.float32),
        jnp.zeros((batch_rows, own_blocks, block_size), jnp.float32),
        jnp.zeros((batch_rows, own_blocks, block_size), jnp.float32),
        jnp.zeros((step_count + 1, batch_rows, own_blocks, gate_width), jnp.bfloat16),
    )
    _, _, _, pre_log = lax.fori_loop(0, wave_count, backward_wave, start)
    pre_used = pre_log[:step_count]
    picked_all = jnp.take(stored[:step_count], flat_layout, axis=1).reshape(
        step_count, own_blocks, nonzero, batch_rows, block_size
    )
    grad_w = jnp.einsum(
        "sjkbc,sbjd->jkcd", picked_all, pre_used, preferred_element_type=jnp.float32
    ).astype(jnp.bfloat16)
    grad_b = jnp.sum(pre_used.astype(jnp.float32), axis=(0, 1))
    return (hidden_log[:step_count][None], grad_w[None], grad_b[None])


def solution(mesh):
    placed = (
        P(),
        P(None, "unit"),
        P("layer", "unit", None, None, None),
        P("layer", "unit", None),
        P("layer", "unit", None),
        P("layer", None, None, "unit"),
    )
    return jax.shard_map(
        on_device,
        mesh=mesh,
        in_specs=placed,
        out_specs=(
            P("layer", None, None, "unit"),
            P("layer", "unit", None, None, None),
            P("layer", "unit", None),
        ),
        check_vma=False,
    )
```

profile of v0, /device:TPU:0, one launch (start us, length us, event | category | flops | bytes accessed | tf_op | source)
XLA Modules:
  0.0 1380.1 jit_solution(13313758475745142503)
XLA Ops:
  12.7 74.1 %all-gather.2.cloned.1.call-done = bf16[256,8192]{0,1:T(8,128)(2,1)} async-done(((bf16[256,1024]{0,1:T(8,128)(2,1)}), bf16[256,8192]{0,1:T(8,128)(2,1)}) %all-gather.2.cloned.1.call-update) | async-done | bytes 4194320 | tf_op jit(solution)/shard_map/all_gather | solution.py:69
  100.5 437.3 %while.47 = (s32[]{:T(128)}, bf16[16,2048]{1,0:T(8,128)(2,1)S(1)}, f32[32,16,64]{2,0,1:T(8,128)}, bf16[5,256,2048]{2,1,0:T(8,128)(2,1)}, f32[5,32,16,64]{3,1,2,0...) while((s32[]{:T(128)}, bf16[16,2048]{1,0:T(8,128)(2,1)S(1)}, ...), condition=%wide.region_1.2_spmd.clone, body=%wide.region_0.1_spmd.clone.sunk | while | flops 678245888 | bytes 56856448 | solution.py:115
  100.5 31.3 %all_gather.14 = bf16[128,2048]{1,0:T(8,128)(2,1)S(1)} all-gather(bf16[16,2048]{1,0:T(8,128)(2,1)S(1)} %broadcast_select_fusion.6), channel_id=1, replica_groups=mesh['layer'=4,'unit'=8] {'unit'}, dimensions={0}, use_global_device_ids=true | all-gather | bytes 589824 | tf_op jit(solution)/shard_map/while/body/eval_jaxpr/all_gather | solution.py:85
  159.6 31.5 %all_gather.14 = bf16[128,2048]{1,0:T(8,128)(2,1)S(1)} all-gather(bf16[16,2048]{1,0:T(8,128)(2,1)S(1)} %broadcast_select_fusion.6), channel_id=1, replica_groups=mesh['layer'=4,'unit'=8] {'unit'}, dimensions={0}, use_global_device_ids=true | all-gather | bytes 589824 | tf_op jit(solution)/shard_map/while/body/eval_jaxpr/all_gather | solution.py:85
  218.9 31.7 %all_gather.14 = bf16[128,2048]{1,0:T(8,128)(2,1)S(1)} all-gather(bf16[16,2048]{1,0:T(8,128)(2,1)S(1)} %broadcast_select_fusion.6), channel_id=1, replica_groups=mesh['layer'=4,'unit'=8] {'unit'}, dimensions={0}, use_global_device_ids=true | all-gather | bytes 589824 | tf_op jit(solution)/shard_map/while/body/eval_jaxpr/all_gather | solution.py:85
  281.6 31.3 %all_gather.14 = bf16[128,2048]{1,0:T(8,128)(2,1)S(1)} all-gather(bf16[16,2048]{1,0:T(8,128)(2,1)S(1)} %broadcast_select_fusion.6), channel_id=1, replica_groups=mesh['layer'=4,'unit'=8] {'unit'}, dimensions={0}, use_global_device_ids=true | all-gather | bytes 589824 | tf_op jit(solution)/shard_map/while/body/eval_jaxpr/all_gather | solution.py:85
  345.7 31.4 %all_gather.14 = bf16[128,2048]{1,0:T(8,128)(2,1)S(1)} all-gather(bf16[16,2048]{1,0:T(8,128)(2,1)S(1)} %broadcast_select_fusion.6), channel_id=1, replica_groups=mesh['layer'=4,'unit'=8] {'unit'}, dimensions={0}, use_global_device_ids=true | all-gather | bytes 589824 | tf_op jit(solution)/shard_map/while/body/eval_jaxpr/all_gather | solution.py:85
  409.8 31.5 %all_gather.14 = bf16[128,2048]{1,0:T(8,128)(2,1)S(1)} all-gather(bf16[16,2048]{1,0:T(8,128)(2,1)S(1)} %broadcast_select_fusion.6), channel_id=1, replica_groups=mesh['layer'=4,'unit'=8] {'unit'}, dimensions={0}, use_global_device_ids=true | all-gather | bytes 589824 | tf_op jit(solution)/shard_map/while/body/eval_jaxpr/all_gather | solution.py:85
  473.8 31.6 %all_gather.14 = bf16[128,2048]{1,0:T(8,128)(2,1)S(1)} all-gather(bf16[16,2048]{1,0:T(8,128)(2,1)S(1)} %broadcast_select_fusion.6), channel_id=1, replica_groups=mesh['layer'=4,'unit'=8] {'unit'}, dimensions={0}, use_global_device_ids=true | all-gather | bytes 589824 | tf_op jit(solution)/shard_map/while/body/eval_jaxpr/all_gather | solution.py:85
  539.0 761.1 %while.48 = (s32[]{:T(128)}, bf16[16,2048]{1,0:T(8,128)(2,1)S(1)}, f32[32,16,64]{2,0,1:T(8,128)S(1)}, f32[32,16,64]{2,0,1:T(8,128)}, bf16[5,32,16,256]{3,1,0,2:T...) while((s32[]{:T(128)}, bf16[16,2048]{1,0:T(8,128)(2,1)S(1)}, ...), condition=%wide.region_5.6_spmd.clone, body=%wide.region_2.5_spmd.clone.sunk | while | flops 541722112 | bytes 44045232 | solution.py:165
  542.4 9.1 collective-permute-done.1
  554.7 17.2 %convolution_bitcast_fusion.2 = f32[16,32,32,64]{3,2,1,0:T(8,128)} fusion(bf16[16,32,64,256]{3,2,1,0:T(8,128)(2,1)} %get-tuple-element.1011, bf16[32,16,64]{2,0,1:T(8,128)(2,1)S(1)} %get-tuple-element.902, bf16[32,16,64]{2,0,1:T(8,128)(2,1)S(1)} %get-tuple-element.904, bf16[32,16,64]{2,0,1:T(8,128)(2,1)S(1)} %get-tuple-element.905, ...), kind=kOutput, calls=%fused_computation.48.clone.1 | convolution fusion | flops 537919488 | bytes 21233664 | tf_op jit(solution)/shard_map/while/body/eval_jaxpr/bjd,jkcd->jkbc/dot_general | solution.py:139
  579.8 8.9 scatter_custom_fusion.6
  590.7 64.1 %reduce-scatter.2.cloned.1.call-done = bf16[2,16,2048]{2,1,0:T(8,128)(2,1)} async-done(((bf16[2,128,2048]{2,1,0:T(8,128)(2,1)}), bf16[2,16,2048]{2,1,0:T(8,128)(2,1)}) %reduce-scatter.2.cloned.1.call-update) | async-done | bytes 131088 | tf_op jit(solution)/shard_map/while/body/eval_jaxpr/reduce_scatter | solution.py:148
  663.6 17.2 %convolution_bitcast_fusion.2 = f32[16,32,32,64]{3,2,1,0:T(8,128)} fusion(bf16[16,32,64,256]{3,2,1,0:T(8,128)(2,1)} %get-tuple-element.1011, bf16[32,16,64]{2,0,1:T(8,128)(2,1)S(1)} %get-tuple-element.902, bf16[32,16,64]{2,0,1:T(8,128)(2,1)S(1)} %get-tuple-element.904, bf16[32,16,64]{2,0,1:T(8,128)(2,1)S(1)} %get-tuple-element.905, ...), kind=kOutput, calls=%fused_computation.48.clone.1 | convolution fusion | flops 537919488 | bytes 21233664 | tf_op jit(solution)/shard_map/while/body/eval_jaxpr/bjd,jkcd->jkbc/dot_general | solution.py:139
  688.6 8.9 scatter_custom_fusion.6
  699.6 62.4 %reduce-scatter.2.cloned.1.call-done = bf16[2,16,2048]{2,1,0:T(8,128)(2,1)} async-done(((bf16[2,128,2048]{2,1,0:T(8,128)(2,1)}), bf16[2,16,2048]{2,1,0:T(8,128)(2,1)}) %reduce-scatter.2.cloned.1.call-update) | async-done | bytes 131088 | tf_op jit(solution)/shard_map/while/body/eval_jaxpr/reduce_scatter | solution.py:148
  770.6 17.2 %convolution_bitcast_fusion.2 = f32[16,32,32,64]{3,2,1,0:T(8,128)} fusion(bf16[16,32,64,256]{3,2,1,0:T(8,128)(2,1)} %get-tuple-element.1011, bf16[32,16,64]{2,0,1:T(8,128)(2,1)S(1)} %get-tuple-element.902, bf16[32,16,64]{2,0,1:T(8,128)(2,1)S(1)} %get-tuple-element.904, bf16[32,16,64]{2,0,1:T(8,128)(2,1)S(1)} %get-tuple-element.905, ...), kind=kOutput, calls=%fused_computation.48.clone.1 | convolution fusion | flops 537919488 | bytes 21233664 | tf_op jit(solution)/shard_map/while/body/eval_jaxpr/bjd,jkcd->jkbc/dot_general | solution.py:139
  806.6 62.6 %reduce-scatter.2.cloned.1.call-done = bf16[2,16,2048]{2,1,0:T(8,128)(2,1)} async-done(((bf16[2,128,2048]{2,1,0:T(8,128)(2,1)}), bf16[2,16,2048]{2,1,0:T(8,128)(2,1)}) %reduce-scatter.2.cloned.1.call-update) | async-done | bytes 131088 | tf_op jit(solution)/shard_map/while/body/eval_jaxpr/reduce_scatter | solution.py:148
  877.9 17.2 %convolution_bitcast_fusion.2 = f32[16,32,32,64]{3,2,1,0:T(8,128)} fusion(bf16[16,32,64,256]{3,2,1,0:T(8,128)(2,1)} %get-tuple-element.1011, bf16[32,16,64]{2,0,1:T(8,128)(2,1)S(1)} %get-tuple-element.902, bf16[32,16,64]{2,0,1:T(8,128)(2,1)S(1)} %get-tuple-element.904, bf16[32,16,64]{2,0,1:T(8,128)(2,1)S(1)} %get-tuple-element.905, ...), kind=kOutput, calls=%fused_computation.48.clone.1 | convolution fusion | flops 537919488 | bytes 21233664 | tf_op jit(solution)/shard_map/while/body/eval_jaxpr/bjd,jkcd->jkbc/dot_general | solution.py:139
  914.0 62.5 %reduce-scatter.2.cloned.1.call-done = bf16[2,16,2048]{2,1,0:T(8,128)(2,1)} async-done(((bf16[2,128,2048]{2,1,0:T(8,128)(2,1)}), bf16[2,16,2048]{2,1,0:T(8,128)(2,1)}) %reduce-scatter.2.cloned.1.call-update) | async-done | bytes 131088 | tf_op jit(solution)/shard_map/while/body/eval_jaxpr/reduce_scatter | solution.py:148
  985.1 17.2 %convolution_bitcast_fusion.2 = f32[16,32,32,64]{3,2,1,0:T(8,128)} fusion(bf16[16,32,64,256]{3,2,1,0:T(8,128)(2,1)} %get-tuple-element.1011, bf16[32,16,64]{2,0,1:T(8,128)(2,1)S(1)} %get-tuple-element.902, bf16[32,16,64]{2,0,1:T(8,128)(2,1)S(1)} %get-tuple-element.904, bf16[32,16,64]{2,0,1:T(8,128)(2,1)S(1)} %get-tuple-element.905, ...), kind=kOutput, calls=%fused_computation.48.clone.1 | convolution fusion | flops 537919488 | bytes 21233664 | tf_op jit(solution)/shard_map/while/body/eval_jaxpr/bjd,jkcd->jkbc/dot_general | solution.py:139
  1010.1 8.9 scatter_custom_fusion.6
  1021.1 62.5 %reduce-scatter.2.cloned.1.call-done = bf16[2,16,2048]{2,1,0:T(8,128)(2,1)} async-done(((bf16[2,128,2048]{2,1,0:T(8,128)(2,1)}), bf16[2,16,2048]{2,1,0:T(8,128)(2,1)}) %reduce-scatter.2.cloned.1.call-update) | async-done | bytes 131088 | tf_op jit(solution)/shard_map/while/body/eval_jaxpr/reduce_scatter | solution.py:148
  1092.3 17.2 %convolution_bitcast_fusion.2 = f32[16,32,32,64]{3,2,1,0:T(8,128)} fusion(bf16[16,32,64,256]{3,2,1,0:T(8,128)(2,1)} %get-tuple-element.1011, bf16[32,16,64]{2,0,1:T(8,128)(2,1)S(1)} %get-tuple-element.902, bf16[32,16,64]{2,0,1:T(8,128)(2,1)S(1)} %get-tuple-element.904, bf16[32,16,64]{2,0,1:T(8,128)(2,1)S(1)} %get-tuple-element.905, ...), kind=kOutput, calls=%fused_computation.48.clone.1 | convolution fusion | flops 537919488 | bytes 21233664 | tf_op jit(solution)/shard_map/while/body/eval_jaxpr/bjd,jkcd->jkbc/dot_general | solution.py:139
  1128.3 62.5 %reduce-scatter.2.cloned.1.call-done = bf16[2,16,2048]{2,1,0:T(8,128)(2,1)} async-done(((bf16[2,128,2048]{2,1,0:T(8,128)(2,1)}), bf16[2,16,2048]{2,1,0:T(8,128)(2,1)}) %reduce-scatter.2.cloned.1.call-update) | async-done | bytes 131088 | tf_op jit(solution)/shard_map/while/body/eval_jaxpr/reduce_scatter | solution.py:148
  1199.5 17.2 %convolution_bitcast_fusion.2 = f32[16,32,32,64]{3,2,1,0:T(8,128)} fusion(bf16[16,32,64,256]{3,2,1,0:T(8,128)(2,1)} %get-tuple-element.1011, bf16[32,16,64]{2,0,1:T(8,128)(2,1)S(1)} %get-tuple-element.902, bf16[32,16,64]{2,0,1:T(8,128)(2,1)S(1)} %get-tuple-element.904, bf16[32,16,64]{2,0,1:T(8,128)(2,1)S(1)} %get-tuple-element.905, ...), kind=kOutput, calls=%fused_computation.48.clone.1 | convolution fusion | flops 537919488 | bytes 21233664 | tf_op jit(solution)/shard_map/while/body/eval_jaxpr/bjd,jkcd->jkbc/dot_general | solution.py:139
  1224.5 8.9 scatter_custom_fusion.6
  1235.5 62.4 %reduce-scatter.2.cloned.1.call-done = bf16[2,16,2048]{2,1,0:T(8,128)(2,1)} async-done(((bf16[2,128,2048]{2,1,0:T(8,128)(2,1)}), bf16[2,16,2048]{2,1,0:T(8,128)(2,1)}) %reduce-scatter.2.cloned.1.call-update) | async-done | bytes 131088 | tf_op jit(solution)/shard_map/while/body/eval_jaxpr/reduce_scatter | solution.py:148
  1313.7 19.4 %gather_fusion.1 = bf16[512,4,2048]{2,1,0:T(4,128)(2,1)} fusion(bf16[4,256,2048]{2,0,1:T(4,128)(2,1)} %slice.128, s32[1024]{0:T(1024)S(1)} %copy-done.9), kind=kCustom, calls=%fused_computation.1 | custom fusion | bytes 16779264 | tf_op jit(solution)/shard_map/jit(_take)/gather | solution.py:167
  1333.1 24.8 %gather.18 = bf16[4,16,32,32,64]{4,3,0,2,1:T(8,128)(2,1)} reshape(bf16[4,512,2048]{2,0,1:T(4,128)(2,1)} %bitcast.178) | data formatting | bytes 16777216 | tf_op jit(solution)/shard_map/jit(_take)/gather | solution.py:167
  1357.9 15.3 %fusion.52 = bf16[1,16,32,64,256]{4,3,2,1,0:T(8,128)(2,1)} fusion(bf16[4,16,32,32,64]{4,3,0,2,1:T(8,128)(2,1)} %gather.18, pred[16,32]{1,0:T(8,128)(4,1)S(1)} %copy-done.8, bf16[5,32,16,256]{3,1,0,2:T(8,128)(2,1)S(1)} %copy-done.6), kind=kOutput, calls=%fused_computation.86 | convolution fusion | flops 2160066560 | bytes 26216448 | tf_op jit(solution)/shard_map/sjkbc,sbjd->jkcd/dot_general | solution.py:170
  (418 shorter events, 405.1 us)
Async XLA Ops:
  7.2 79.7 %all-gather.2.cloned.1.call-start = ((), (), s32[]{:S(2)}) async-start(), calls=%async_computation.1 | async-start | bytes 4718592 | tf_op jit(solution)/shard_map/all_gather | solution.py:69
  131.8 5.6 collective-permute-start
  146.3 8.7 copy-start.4
  191.1 5.6 collective-permute-start
  250.6 8.9 copy-start
  250.6 8.8 collective-permute-start
  268.3 8.7 copy-start.4
  312.9 10.6 copy-start
  312.9 10.6 collective-permute-start
  377.1 10.6 copy-start
  377.1 10.6 collective-permute-start
  441.3 10.4 copy-start
  441.3 10.4 collective-permute-start
  460.5 8.7 copy-start.4
  505.5 10.2 copy-start
  505.5 10.2 collective-permute-start
  539.0 115.9 %reduce-scatter.2.cloned.1.call-start = ((), (), s32[]{:S(2)}) async-start(), calls=%async_computation.2 | async-start | bytes 1179648 | tf_op jit(solution)/shard_map/while/body/eval_jaxpr/reduce_scatter | solution.py:148
  539.0 12.5 collective-permute-start.1
  656.8 105.2 %reduce-scatter.2.cloned.1.call-start = ((), (), s32[]{:S(2)}) async-start(), calls=%async_computation.2 | async-start | bytes 1179648 | tf_op jit(solution)/shard_map/while/body/eval_jaxpr/reduce_scatter | solution.py:148
  656.9 3.4 collective-permute-start.1
  763.9 105.3 %reduce-scatter.2.cloned.1.call-start = ((), (), s32[]{:S(2)}) async-start(), calls=%async_computation.2 | async-start | bytes 1179648 | tf_op jit(solution)/shard_map/while/body/eval_jaxpr/reduce_scatter | solution.py:148
  764.0 3.4 collective-permute-start.1
  871.2 105.3 %reduce-scatter.2.cloned.1.call-start = ((), (), s32[]{:S(2)}) async-start(), calls=%async_computation.2 | async-start | bytes 1179648 | tf_op jit(solution)/shard_map/while/body/eval_jaxpr/reduce_scatter | solution.py:148
  871.2 3.4 collective-permute-start.1
  978.4 105.2 %reduce-scatter.2.cloned.1.call-start = ((), (), s32[]{:S(2)}) async-start(), calls=%async_computation.2 | async-start | bytes 1179648 | tf_op jit(solution)/shard_map/while/body/eval_jaxpr/reduce_scatter | solution.py:148
  978.4 3.4 collective-permute-start.1
  1085.5 105.3 %reduce-scatter.2.cloned.1.call-start = ((), (), s32[]{:S(2)}) async-start(), calls=%async_computation.2 | async-start | bytes 1179648 | tf_op jit(solution)/shard_map/while/body/eval_jaxpr/reduce_scatter | solution.py:148
  1085.6 3.4 collective-permute-start.1
  1192.8 105.2 %reduce-scatter.2.cloned.1.call-start = ((), (), s32[]{:S(2)}) async-start(), calls=%async_computation.2 | async-start | bytes 1179648 | tf_op jit(solution)/shard_map/while/body/eval_jaxpr/reduce_scatter | solution.py:148
  1192.8 3.4 collective-permute-start.1
  1333.1 24.8 %copy-start.6 = (bf16[5,32,16,256]{3,1,0,2:T(8,128)(2,1)S(1)}, bf16[5,32,16,256]{3,1,0,2:T(8,128)(2,1)}, u32[]{:S(2)}) copy-start(bf16[5,32,16,256]{3,1,0,2:T(8,128)(2,1)} %get-tuple-element.566) | copy-start | bytes 3932164
  1333.1 24.8 %copy-start.8 = (pred[16,32]{1,0:T(8,128)(4,1)S(1)}, pred[16,32]{1,0:T(8,128)(4,1)}, u32[]{:S(2)}) copy-start(pred[16,32]{1,0:T(8,128)(4,1)} %compare_and_fusion.1) | copy-start | bytes 1540
  (36 other events, 109.0 us)
Sparse Core Ops, SparseCore 0:
  10.7 76.0 all-gather.1
  590.0 64.8 reduce-scatter.1
  698.8 63.1 reduce-scatter.1
  805.9 63.3 reduce-scatter.1
  913.2 63.2 reduce-scatter.1
  1020.4 63.2 reduce-scatter.1
  1127.5 63.2 reduce-scatter.1
  1234.7 63.1 reduce-scatter.1
where the time goes:
time: 1390 us; the launch traced here: 1380 us
  waiting for transfers between devices  522 us (38%)
  local copies, waits for them, and re-layouts  221 us (16%)
  blocking collectives  220 us (16%)
  matrix products  218 us (16%)
  other arithmetic  141 us (10%)
  starting transfers between devices  40.9 us (3%)
  between operations  14.1 us (1%)
    reduce_scatter x7, waiting for transfers between devices, backward_wave(): lax.psum_scatter(halves.astype(jnp.bfloat16), 'unit', scatter_dimension=1...  439 us
    all_gather x7, blocking collectives, forward_wave(): hidden_full = lax.all_gather(hidden_own, 'unit', axis=0, tiled=True)  220 us
    dot_general x7, matrix products, backward_wave(): jnp.einsum('bjd,jkcd->jkbc', grad_pre, weight_blocks, preferred_element_t...  120 us
    all_gather x1, waiting for transfers between devices, on_device(): lax.all_gather(embed, 'unit', axis=1, tiled=True)  74.1 us
    scatter-add x7, other arithmetic, backward_wave(): partial_value = jnp.zeros((2 * all_blocks, row_width), jnp.float32).at[fl...  62.6 us
    dot_general x7, matrix products, forward_wave(): jnp.einsum('jkbc,jkcd->bjd', picked, weight_blocks, preferred_element_typ...  60.7 us
    gather x14, local copies, waits for them, and re-layouts, forward_wave(): jnp.take(inputs, flat_layout, axis=0)  55.1 us
    reshape x7, local copies, waits for them, and re-layouts, backward_wave(): contrib.reshape(own_blocks * nonzero, row_width)  54.9 us
  transfers between devices with their start and end apart: 22, of which 9 were waited for; matrix products, arithmetic and copies ran while one was open for 4% of the time, Pallas kernels for 0%

commit v1 on v0

v1 whole, which is shorter than its diff:
```python
import functools

import jax
import jax.numpy as jnp
from jax import lax
from jax.experimental import pallas as pl
from jax.experimental.pallas import tpu as pltpu
from jax.sharding import PartitionSpec as P

MESH = pl.DeviceIdType.MESH
F32 = jnp.float32
BF16 = jnp.bfloat16
INNER = 2


def looped(count, unroll, body):
    while count % unroll:
        unroll -= 1

    def several(step, carry):
        for part in range(unroll):
            body(step * unroll + part)
        return carry

    lax.fori_loop(0, count // unroll, several, 0)


def lstm_kernel(
    layers,
    units,
    groups,
    lay_ref,
    perm_ref,
    same_ref,
    last_ref,
    emb_ref,
    w_hbm,
    bias_ref,
    cot_ref,
    hid_ref,
    g_hbm,
    gp_ref,
    w_ref,
    g_ref,
    x_ref,
    h_ref,
    s_ref,
    act_ref,
    cell_ref,
    c_ref,
    r_ref,
    p_ref,
    xr_ref,
    zr_ref,
    q_ref,
    d_ref,
    ds_ref,
    rec_ref,
    carry_ref,
    w_sem,
    g_sem,
    h_recv,
    s_recv,
    z_send,
    x_send,
    up_send,
    ez_send,
    ex_send,
    xr_recv,
    zr_recv,
    xr_send,
    zr_send,
    d_recv,
    d_send,
):
    layer = lax.axis_index("layer")
    unit = lax.axis_index("unit")
    outer = units // INNER
    zpos = unit // INNER
    xpos = unit % INNER
    partner = zpos * INNER + (1 - xpos)
    steps, rows, _ = cot_ref.shape
    own_blocks, nonzero = lay_ref.shape
    pairs = own_blocks // 2
    half_blocks = units * own_blocks
    entries = own_blocks * nonzero // groups
    per_group = own_blocks // groups
    has_above = layer < layers - 1
    has_below = layer > 0
    low = lax.broadcasted_iota(jnp.int32, (rows, 128), 1) < 64

    def other_z(dz):
        return lax.rem(zpos + dz, outer)

    def swap(tile):
        return pltpu.roll(tile, 64, axis=1)

    def remote(src, dst, send, recv, where_to):
        return pltpu.make_async_remote_copy(
            src_ref=src,
            dst_ref=dst,
            send_sem=send,
            recv_sem=recv,
            device_id=where_to,
            device_id_type=MESH,
        )

    barrier = pltpu.get_barrier_semaphore()

    def greet(where_to):
        pl.semaphore_signal(barrier, inc=1, device_id=where_to, device_id_type=MESH)

    for dz in range(1, outer):
        greet((layer, other_z(dz) * INNER + xpos))
    greet((layer, partner))

    @pl.when(has_above)
    def _():
        greet((layer + 1, unit))

    @pl.when(has_below)
    def _():
        greet((layer - 1, unit))

    pl.semaphore_wait(
        barrier, outer + lax.min(layers - 1 - layer, 1) + lax.min(layer, 1)
    )

    def emb_z(t, dz):
        return remote(
            s_ref.at[t, unit],
            s_ref.at[t, unit],
            ez_send.at[t, dz],
            s_recv.at[t, unit],
            (layer, other_z(dz) * INNER + xpos),
        )

    def emb_x(t, dz):
        v = other_z(dz) * INNER + xpos
        return remote(
            s_ref.at[t, v], s_ref.at[t, v], ex_send.at[t, dz], s_recv.at[t, v], (layer, partner)
        )

    def s_wait(t, v):
        remote(
            s_ref.at[t, v], s_ref.at[t, v], ex_send.at[t, 0], s_recv.at[t, v], (layer, partner)
        ).wait_recv()

    def emb_forward(t):
        for dz in range(1, outer):
            s_wait(t, other_z(dz) * INNER + xpos)
            emb_x(t, dz).start()

    @pl.when(layer == 0)
    def _():
        for t in range(steps):
            s_ref[t, unit] = emb_ref[t]
            for dz in range(1, outer):
                emb_z(t, dz).start()
            emb_x(t, 0).start()

    def w_copy(j):
        return pltpu.make_async_copy(w_hbm.at[j], w_ref.at[j], w_sem.at[j])

    looped(own_blocks, 1, lambda j: w_copy(j).start())

    zero_tile = jnp.zeros((rows, 128), F32)

    def zero_x(b):
        x_ref[half_blocks + b] = jnp.zeros((rows, 128), BF16)

    looped(half_blocks, 8, zero_x)
    for q in range(pairs):
        rec_ref[q] = zero_tile
        carry_ref[q] = zero_tile
        cell_ref[0, q] = zero_tile
    for g in range(groups):
        r_ref[g * (entries + 1) + entries] = zero_tile

    @pl.when(layer == layers - 1)
    def _():
        for t in range(steps):
            for q in range(pairs):
                d_ref[t, q] = jnp.zeros((rows, 128), BF16)

    def unpack(src, t, v, base):
        for q in range(pairs):
            tile = src[t, v, q].astype(F32)
            turned = swap(tile)
            at = base + v * own_blocks + 2 * q
            x_ref[at] = jnp.where(low, tile, turned).astype(BF16)
            x_ref[at + 1] = jnp.where(low, turned, tile).astype(BF16)

    @pl.when(layer == 0)
    def _():
        emb_forward(0)

    looped(own_blocks, 1, lambda j: w_copy(j).wait())

    def own_copy_z(t, dz):
        return remote(
            h_ref.at[t, unit],
            h_ref.at[t, unit],
            z_send.at[dz],
            h_recv.at[t, unit],
            (layer, other_z(dz) * INNER + xpos),
        )

    def copy_x(t, dz):
        v = other_z(dz) * INNER + xpos
        return remote(
            h_ref.at[t, v], h_ref.at[t, v], x_send.at[dz], h_recv.at[t, v], (layer, partner)
        )

    def copy_up(t, v):
        return remote(
            h_ref.at[t, v], s_ref.at[t, v], up_send.at[v], s_recv.at[t, v], (layer + 1, unit)
        )

    def h_wait(t, v):
        remote(
            h_ref.at[t, v], h_ref.at[t, v], x_send.at[0], h_recv.at[t, v], (layer, partner)
        ).wait_recv()

    def wait_up(t):
        @pl.when((layers - 1 - layer) * (t + 1) > 0)
        def _():
            looped(units, 1, lambda v: copy_up(t, v).wait_send())

    def forward(t, carry):
        def take_source(i):
            v = lax.rem(unit + i, units)

            @pl.when(layer + lax.abs(lax.rem(v, INNER) - xpos) > 0)
            def _():
                s_wait(t, v)

            unpack(s_ref, t, v, 0)

        looped(units, 1, take_source)

        def cells(q):
            pres = []
            for side in range(2):
                j = 2 * q + side
                tiles = []
                for k in range(0, nonzero, 2):
                    tiles.append(
                        jnp.where(low, x_ref[lay_ref[j, k]], x_ref[lay_ref[j, k + 1]])
                    )
                picked = jnp.concatenate(tiles, axis=1)
                g_ref[j, pl.ds(pl.multiple_of(t * rows, rows), rows), :] = picked
                pres.append(
                    jnp.dot(picked, w_ref[j], preferred_element_type=F32)
                    + bias_ref[pl.ds(j, 1), :]
                )
            first, second = pres
            i_pre = jnp.where(low, first[:, :128], swap(second[:, :128]))
            f_pre = jnp.where(low, swap(first[:, :128]), second[:, :128])
            u_pre = jnp.where(low, first[:, 128:], swap(second[:, 128:]))
            o_pre = jnp.where(low, swap(first[:, 128:]), second[:, 128:])
            in_gate = jax.nn.sigmoid(i_pre)
            forget = jax.nn.sigmoid(f_pre)
            update = jnp.tanh(u_pre)
            out_gate = jax.nn.sigmoid(o_pre)
            cell = forget * cell_ref[t, q] + in_gate * update
            squash = jnp.tanh(cell)
            hidden = (out_gate * squash).astype(BF16)
            cell_ref[t + 1, q] = cell
            act_ref[0, t, q] = in_gate
            act_ref[1, t, q] = forget
            act_ref[2, t, q] = update
            act_ref[3, t, q] = out_gate
            act_ref[4, t, q] = squash
            h_ref[t, unit, q] = hidden
            hid_ref[t, :, pl.ds(pl.multiple_of(q * 128, 128), 128)] = hidden

        looped(pairs, 2, cells)

        wait_up(t - 1)

        @pl.when((layers - 1 - layer) + (steps - 1 - t) > 0)
        def _():
            for dz in range(1, outer):
                own_copy_z(t, dz).start()
            copy_x(t, 0).start()

            @pl.when(has_above)
            def _():
                copy_up(t, unit).start()

            @pl.when(layer + lax.div(t + 1, steps) == 0)
            def _():
                emb_forward(t + 1)

            unpack(h_ref, t, unit, half_blocks)

            def arrived(dz, is_partner):
                v = other_z(dz) * INNER + (1 - xpos if is_partner else xpos)
                h_wait(t, v)
                if not is_partner:
                    copy_x(t, dz).start()

                @pl.when(has_above)
                def _():
                    copy_up(t, v).start()

                unpack(h_ref, t, v, half_blocks)

            looped(outer - 1, 1, lambda i: arrived(i + 1, False))
            looped(outer, 1, lambda i: arrived(i, True))
            for dz in range(1, outer):
                own_copy_z(t, dz).wait_send()
            for dz in range(outer):
                copy_x(t, dz).wait_send()

        return carry

    lax.fori_loop(0, steps, forward, 0)
    g_copy = pltpu.make_async_copy(g_ref, g_hbm, g_sem)
    g_copy.start()
    wait_up(steps - 1)

    @pl.when(layer == 0)
    def _():
        for t in range(steps):
            for dz in range(1, outer):
                emb_z(t, dz).wait_send()
            for dz in range(outer):
                emb_x(t, dz).wait_send()

    def group_sum(half, v, q):
        at = half * half_blocks + v * own_blocks + 2 * q
        left = right = None
        for g in range(groups):
            one = r_ref[last_ref[g, at]]
            two = r_ref[last_ref[g, at + 1]]
            left = one if left is None else left + one
            right = two if right is None else right + two
        return jnp.where(low, left, right)

    def copy_xr(t, half, z):
        return remote(
            p_ref.at[half, z],
            xr_ref.at[t, half, z],
            xr_send.at[half, z],
            xr_recv.at[t, half, z],
            (layer, partner),
        )

    def copy_zr(t, half, dz):
        z = other_z(dz)
        return remote(
            q_ref.at[half, z],
            zr_ref.at[t, half, zpos],
            zr_send.at[half, z],
            zr_recv.at[t, half, zpos],
            (layer, z * INNER + xpos),
        )

    def wait_zr(t, half, dz):
        z = other_z(dz)
        remote(
            q_ref.at[half, z],
            zr_ref.at[t, half, z],
            zr_send.at[half, z],
            zr_recv.at[t, half, z],
            (layer, z * INNER + xpos),
        ).wait_recv()

    def copy_down(t):
        return remote(ds_ref, d_ref.at[t], d_send, d_recv.at[t], (layer - 1, unit))

    def backward(i, carry):
        t = steps - 1 - i

        @pl.when(has_above)
        def _():
            remote(ds_ref, d_ref.at[t], d_send, d_recv.at[t], (layer + 1, unit)).wait_recv()

        def cells(q):
            grad_hidden = (
                cot_ref[t, :, pl.ds(pl.multiple_of(q * 128, 128), 128)].astype(F32)
                + d_ref[t, q].astype(F32)
                + rec_ref[q]
            )
            in_gate = act_ref[0, t, q]
            forget = act_ref[1, t, q]
            update = act_ref[2, t, q]
            out_gate = act_ref[3, t, q]
            squash = act_ref[4, t, q]
            grad_cell = carry_ref[q] + grad_hidden * out_gate * (1.0 - squash * squash)
            gi = grad_cell * update * in_gate * (1.0 - in_gate)
            gf = grad_cell * cell_ref[t, q] * forget * (1.0 - forget)
            gu = grad_cell * in_gate * (1.0 - update * update)
            go = grad_hidden * squash * out_gate * (1.0 - out_gate)
            carry_ref[q] = grad_cell * forget
            at = pl.ds(pl.multiple_of(t * rows, rows), rows)
            gp_ref[2 * q, at, :128] = jnp.where(low, gi, swap(gf)).astype(BF16)
            gp_ref[2 * q, at, 128:] = jnp.where(low, gu, swap(go)).astype(BF16)
            gp_ref[2 * q + 1, at, :128] = jnp.where(low, swap(gi), gf).astype(BF16)
            gp_ref[2 * q + 1, at, 128:] = jnp.where(low, swap(gu), go).astype(BF16)

        looped(pairs, 2, cells)

        @pl.when(layer + t > 0)
        def _():
            def two_groups(gg, inner_carry):
                def contributions(jl):
                    j = gg * (2 * per_group) + jl
                    grad_pre = gp_ref[j, pl.ds(pl.multiple_of(t * rows, rows), rows), :]
                    contrib = lax.dot_general(
                        grad_pre, w_ref[j], (((1,), (1,)), ((), ())), preferred_element_type=F32
                    )
                    for k in range(0, nonzero, 2):
                        tile = contrib[:, k * 64 : k * 64 + 128]
                        turned = swap(tile)
                        c_ref[jl * nonzero + k] = jnp.where(low, tile, turned)
                        c_ref[jl * nonzero + k + 1] = jnp.where(low, turned, tile)

                looped(2 * per_group, 2, contributions)

                def runs(r8, run):
                    run = list(run)
                    for part in range(8):
                        r = r8 * 8 + part
                        for side in range(2):
                            g = gg * 2 + side
                            run[side] = c_ref[perm_ref[g, r]] + same_ref[g, r] * run[side]
                            r_ref[g * (entries + 1) + r] = run[side]
                    return tuple(run)

                lax.fori_loop(0, entries // 8, runs, (zero_tile, zero_tile))
                return inner_carry

            lax.fori_loop(0, groups // 2, two_groups, 0)

            def per_half(do):
                @pl.when(t > 0)
                def _():
                    do(1)

                @pl.when(has_below)
                def _():
                    do(0)

            def send_partner(half):
                def one(i):
                    z = other_z(lax.rem(i + 1, outer))
                    for q in range(pairs):
                        p_ref[half, z, q] = group_sum(
                            half, z * INNER + (1 - xpos), q
                        ).astype(BF16)
                    copy_xr(t, half, z).start()

                looped(outer, 1, one)

            def send_along(half):
                def one(i):
                    dz = i + 1
                    z = other_z(dz)
                    copy_xr(t, half, z).wait_recv()
                    for q in range(pairs):
                        q_ref[half, z, q] = (
                            group_sum(half, z * INNER + xpos, q)
                            + xr_ref[t, half, z, q].astype(F32)
                        ).astype(BF16)
                    copy_zr(t, half, dz).start()

                looped(outer - 1, 1, one)

            def finish(half):
                copy_xr(t, half, zpos).wait_recv()
                for dz in range(1, outer):
                    wait_zr(t, half, dz)

                def one(q):
                    total = group_sum(half, unit, q) + xr_ref[t, half, zpos, q].astype(F32)
                    for dz in range(1, outer):
                        total = total + zr_ref[t, half, other_z(dz), q].astype(F32)
                    if half:
                        rec_ref[q] = total
                    else:
                        ds_ref[q] = total.astype(BF16)

                looped(pairs, 2, one)
                if not half:
                    copy_down(t).start()

            def settle(half):
                for z in range(outer):
                    copy_xr(t, half, z).wait_send()
                for dz in range(1, outer):
                    copy_zr(t, half, dz).wait_send()
                if not half:
                    copy_down(t).wait_send()

            per_half(send_partner)
            per_half(send_along)
            per_half(finish)
            per_half(settle)

        return carry

    lax.fori_loop(0, steps, backward, 0)
    g_copy.wait()


def weight_kernel(g_ref, gp_ref, gw_ref, gb_ref):
    grad_pre = gp_ref[0]
    gw_ref[0] = lax.dot_general(
        g_ref[0], grad_pre, (((0,), (0,)), ((), ())), preferred_element_type=F32
    ).astype(BF16)
    gb_ref[0] = jnp.sum(grad_pre.astype(F32), axis=0, keepdims=True)


def on_device(layers, units, tokens, embed, weights, layout, bias, d_hidden):
    steps, rows = tokens.shape
    vocab, width = embed.shape
    _, own_blocks, nonzero, block, gates = weights.shape
    pairs = own_blocks // 2
    half_blocks = units * own_blocks
    groups = 4 if own_blocks % 4 == 0 else 2
    entries = own_blocks * nonzero // groups
    outer = units // INNER
    depth = nonzero * block

    onehot = (tokens.reshape(-1)[:, None] == jnp.arange(vocab, dtype=jnp.int32)).astype(BF16)
    looked = jnp.dot(onehot, embed, preferred_element_type=F32).astype(BF16)
    emb = looked.reshape(steps, rows, pairs, 128).transpose(0, 2, 1, 3)

    lay = layout[0]
    ent = lay.reshape(groups, entries)
    spot = jnp.arange(entries, dtype=jnp.int32)
    key = ent * entries + spot
    rank = jnp.sum((key[:, None, :] < key[:, :, None]).astype(jnp.int32), -1)
    placed = rank[:, :, None] == spot
    perm = jnp.sum(jnp.where(placed, spot[:, None], 0), 1)
    ordered = jnp.sum(jnp.where(placed, ent[:, :, None], 0), 1)
    same = jnp.concatenate(
        [jnp.zeros((groups, 1), F32), (ordered[:, 1:] == ordered[:, :-1]).astype(F32)], 1
    )
    group_ids = jnp.arange(groups, dtype=jnp.int32)[:, None]
    perm = perm + (group_ids % 2) * entries
    blocks = jnp.arange(2 * half_blocks, dtype=jnp.int32)[:, None]
    below = jnp.sum((ent[:, None, :] <= blocks).astype(jnp.int32), -1)
    present = jnp.any(ent[:, None, :] == blocks, -1)
    last = jnp.where(present, below - 1, entries) + group_ids * (entries + 1)

    smem = pl.BlockSpec(memory_space=pltpu.SMEM)
    vmem = pl.BlockSpec(memory_space=pltpu.VMEM)
    hbm = pl.BlockSpec(memory_space=pl.ANY)
    tile = (rows, 128)
    dma = pltpu.SemaphoreType.DMA
    hidden, picked, grad_pre = pl.pallas_call(
        functools.partial(lstm_kernel, layers, units, groups),
        out_shape=(
            jax.ShapeDtypeStruct((steps, rows, width), BF16),
            jax.ShapeDtypeStruct((own_blocks, steps * rows, depth), BF16),
            jax.ShapeDtypeStruct((own_blocks, steps * rows, gates), BF16),
        ),
        in_specs=[smem, smem, smem, smem, vmem, hbm, vmem, vmem],
        out_specs=(vmem, hbm, vmem),
        scratch_shapes=[
            pltpu.VMEM((own_blocks, depth, gates), BF16),
            pltpu.VMEM((own_blocks, steps * rows, depth), BF16),
            pltpu.VMEM((2 * half_blocks,) + tile, BF16),
            pltpu.VMEM((steps, units, pairs) + tile, BF16),
            pltpu.VMEM((steps, units, pairs) + tile, BF16),
            pltpu.VMEM((5, steps, pairs) + tile, F32),
            pltpu.VMEM((steps + 1, pairs) + tile, F32),
            pltpu.VMEM((2 * entries,) + tile, F32),
            pltpu.VMEM((groups * (entries + 1),) + tile, F32),
            pltpu.VMEM((2, outer, pairs) + tile, BF16),
            pltpu.VMEM((steps, 2, outer, pairs) + tile, BF16),
            pltpu.VMEM((steps, 2, outer, pairs) + tile, BF16),
            pltpu.VMEM((2, outer, pairs) + tile, BF16),
            pltpu.VMEM((steps, pairs) + tile, BF16),
            pltpu.VMEM((pairs,) + tile, BF16),
            pltpu.VMEM((pairs,) + tile, F32),
            pltpu.VMEM((pairs,) + tile, F32),
            dma((own_blocks,)),
            dma,
            dma((steps, units)),
            dma((steps, units)),
            dma((outer,)),
            dma((outer,)),
            dma((units,)),
            dma((steps, outer)),
            dma((steps, outer)),
            dma((steps, 2, outer)),
            dma((steps, 2, outer)),
            dma((2, outer)),
            dma((2, outer)),
            dma((steps,)),
            dma,
        ],
        compiler_params=pltpu.CompilerParams(
            collective_id=0, has_side_effects=True, vmem_limit_bytes=60 * 2**20
        ),
        name="lstm",
    )(lay, perm, same, last, emb, weights[0].reshape(own_blocks, depth, gates), bias[0], d_hidden[0])

    grad_w, grad_b = pl.pallas_call(
        weight_kernel,
        grid=(own_blocks,),
        out_shape=(
            jax.ShapeDtypeStruct((own_blocks, depth, gates), BF16),
            jax.ShapeDtypeStruct((own_blocks, 1, gates), F32),
        ),
        in_specs=[
            pl.BlockSpec((1, steps * rows, depth), lambda j: (j, 0, 0)),
            pl.BlockSpec((1, steps * rows, gates), lambda j: (j, 0, 0)),
        ],
        out_specs=(
            pl.BlockSpec((1, depth, gates), lambda j: (j, 0, 0)),
            pl.BlockSpec((1, 1, gates), lambda j: (j, 0, 0)),
        ),
        name="grad_weights",
    )(picked, grad_pre)
    return (
        hidden[None],
        grad_w.reshape(1, own_blocks, nonzero, block, gates),
        grad_b.reshape(1, own_blocks, gates),
    )


def solution(mesh):
    placed = (
        P(),
        P(None, "unit"),
        P("layer", "unit", None, None, None),
        P("layer", "unit", None),
        P("layer", "unit", None),
        P("layer", None, None, "unit"),
    )
    return jax.shard_map(
        functools.partial(on_device, mesh.shape["layer"], mesh.shape["unit"]),
        mesh=mesh,
        in_specs=placed,
        out_specs=(
            P("layer", None, None, "unit"),
            P("layer", "unit", None, None, None),
            P("layer", "unit", None),
        ),
        check_vma=False,
    )
```

time: 1390 us -> 288 us (0.21)
  waiting for transfers between devices: 522 us -> 0 us
  Pallas kernels: 0 us -> 278 us
  blocking collectives: 220 us -> 0 us
  matrix products: 218 us -> 0.26 us
  local copies, waits for them, and re-layouts: 221 us -> 5.39 us
  other arithmetic: 141 us -> 2.97 us
  starting transfers between devices: 40.9 us -> 0 us
    reduce_scatter x7 -> x0, waiting for transfers between devices: 439 us -> none  [backward_wave(): lax.psum_scatter(halves.astype(jnp.bfloat16), 'unit', scatter_dimension=1...]
    pallas_call x0 -> x2, Pallas kernels: none -> 278 us  [the longest x1 261 us: on_device(): pl.pallas_call(functools.partial(lstm_kernel, layers, units, groups), out...]
    all_gather x7 -> x0, blocking collectives: 220 us -> none  [forward_wave(): hidden_full = lax.all_gather(hidden_own, 'unit', axis=0, tiled=True)]
    dot_general x22 -> x1, matrix products: 218 us -> 0.26 us  [on_device(): looked = jnp.dot(onehot, embed, preferred_element_type=F32).astype(BF16)]
    gather x16 -> x0, local copies, waits for them, and re-layouts: 99.3 us -> none  [the longest x14 55.1 us: forward_wave(): jnp.take(inputs, flat_layout, axis=0)]
    all_gather x1 -> x0, waiting for transfers between devices: 74.1 us -> none  [on_device(): lax.all_gather(embed, 'unit', axis=1, tiled=True)]
    scatter-add x7 -> x0, other arithmetic: 62.6 us -> none  [backward_wave(): partial_value = jnp.zeros((2 * all_blocks, row_width), jnp.float32).at[fl...]
    reshape x21 -> x1, local copies, waits for them, and re-layouts: 57.7 us -> 0.75 us  [on_device(): emb = looked.reshape(steps, rows, pairs, 128).transpose(0, 2, 1, 3)]
  transfers between devices with their start and end apart: 22 -> 0, of which waited for: 9 -> 0; matrix products, arithmetic and copies ran while one was open for 4% -> 0% of each run, Pallas kernels for 0% -> 0%
where the time goes in v1:
time: 288 us; the launch traced here: 287 us
  Pallas kernels  278 us (97%)
  local copies, waits for them, and re-layouts  5.39 us (2%)
  other arithmetic  2.97 us (1%)
    pallas_call x1, Pallas kernels, on_device(): pl.pallas_call(functools.partial(lstm_kernel, layers, units, groups), out...  261 us
    pallas_call x1, Pallas kernels, on_device(): pl.pallas_call(weight_kernel, grid=(own_blocks,), out_shape=(jax.ShapeDty...  16.6 us

profile of v1, /device:TPU:0, one launch (start us, length us, event | category | flops | bytes accessed | tf_op | source)
XLA Modules:
  0.0 286.9 jit_solution(5162254332670378697)
XLA Ops:
  0.6 0.0 copy-start
  0.6 0.8 eq.56
  1.5 0.8 reshape_squeeze.6
  2.2 0.2 fusion.1
  2.5 0.2 convert_reduce_fusion.1
  2.7 0.2 select_reduce_fusion
  2.9 0.1 slice_compare_fusion
  3.0 0.7 pad_convert_fusion.same_ref
  3.7 0.6 broadcast_add_fusion.perm_ref
  4.3 0.2 convert_reduce_fusion
  4.6 0.7 select_add_fusion.last_ref
  5.2 0.0 copy-done
  5.2 0.3 fusion
  5.6 0.7 copy.16
  6.3 261.0 %lstm.1 = (bf16[4,32,1024]{2,1,0:T(8,128)(2,1)}, bf16[16,128,2048]{2,1,0:T(8,128)(2,1)}, bf16[16,128,256]{2,1,0:T(8,128)(2,1)}) custom-call(s32[16,32]{1,0:T(8,128)} %bitcast.20, s32[4,128]{1,0:T(4,128)} %broadcast_add_fusion.perm_ref, f32[4,128]{1,0:T(4,128)} %pad_convert_fusion.same_ref, s32[4,256]{1,0:T(4,128)} %select_add_fusion.last_ref, ...), custom_call_target="tpu_custom_call" | custom-call | tf_op jit(solution)/shard_map/lstm/pallas_call | solution.py:555
  267.3 16.6 %grad_weights.1 = (bf16[16,2048,256]{2,1,0:T(8,128)(2,1)}, f32[16,1,256]{2,1,0:T(1,128)}) custom-call(bf16[16,128,2048]{2,1,0:T(8,128)(2,1)} %get-tuple-element.9.g_ref, bf16[16,128,256]{2,1,0:T(8,128)(2,1)} %get-tuple-element.10.gp_ref), custom_call_target="tpu_custom_call" | custom-call | tf_op jit(solution)/shard_map/grad_weights/pallas_call | solution.py:604
  283.9 1.3 copy.13
  285.3 1.7 copy.18
  (4 shorter events, 0.1 us)
Async XLA Ops:
  0.6 4.6 %copy-start = (bf16[256,1024]{1,0:T(8,128)(2,1)S(1)}, bf16[256,1024]{1,0:T(8,128)(2,1)}, u32[]{:S(2)}) copy-start(bf16[256,1024]{1,0:T(8,128)(2,1)} %param.7) | copy-start | bytes 1572868

commit v2 on v1

--- a/solution.py
+++ b/solution.py
@@ -11,6 +11,7 @@
 F32 = jnp.float32
 BF16 = jnp.bfloat16
 INNER = 2
+SUBS = 2
 
 
 def looped(count, unroll, body):
@@ -38,10 +39,10 @@
     bias_ref,
     cot_ref,
     hid_ref,
-    g_hbm,
+    xt_hbm,
     gp_ref,
     w_ref,
-    g_ref,
+    xt_ref,
     x_ref,
     h_ref,
     s_ref,
@@ -58,7 +59,7 @@
     rec_ref,
     carry_ref,
     w_sem,
-    g_sem,
+    xt_sem,
     h_recv,
     s_recv,
     z_send,
@@ -82,6 +83,7 @@
     steps, rows, _ = cot_ref.shape
     own_blocks, nonzero = lay_ref.shape
     pairs = own_blocks // 2
+    sub_pairs = pairs // SUBS
     half_blocks = units * own_blocks
     entries = own_blocks * nonzero // groups
     per_group = own_blocks // groups
@@ -126,38 +128,44 @@
         barrier, outer + lax.min(layers - 1 - layer, 1) + lax.min(layer, 1)
     )
 
-    def emb_z(t, dz):
+    def part(ref, t, v, sub):
+        return ref.at[t, v, pl.ds(sub * sub_pairs, sub_pairs)]
+
+    def emb_z(t, dz, sub):
+        here = part(s_ref, t, unit, sub)
         return remote(
-            s_ref.at[t, unit],
-            s_ref.at[t, unit],
-            ez_send.at[t, dz],
-            s_recv.at[t, unit],
+            here,
+            here,
+            ez_send.at[t, dz, sub],
+            s_recv.at[t, unit, sub],
             (layer, other_z(dz) * INNER + xpos),
         )
 
-    def emb_x(t, dz):
+    def emb_x(t, dz, sub):
         v = other_z(dz) * INNER + xpos
-        return remote(
-            s_ref.at[t, v], s_ref.at[t, v], ex_send.at[t, dz], s_recv.at[t, v], (layer, partner)
-        )
-
-    def s_wait(t, v):
+        here = part(s_ref, t, v, sub)
+        return remote(here, here, ex_send.at[t, dz, sub], s_recv.at[t, v, sub], (layer, partner))
+
+    def s_wait(t, v, sub):
+        here = part(s_ref, t, v, sub)
         remote(
-            s_ref.at[t, v], s_ref.at[t, v], ex_send.at[t, 0], s_recv.at[t, v], (layer, partner)
+            here, here, ex_send.at[t, 0, sub], s_recv.at[t, v, sub], (layer, partner)
         ).wait_recv()
 
     def emb_forward(t):
-        for dz in range(1, outer):
-            s_wait(t, other_z(dz) * INNER + xpos)
-            emb_x(t, dz).start()
+        for sub in range(SUBS):
+            for dz in range(1, outer):
+                s_wait(t, other_z(dz) * INNER + xpos, sub)
+                emb_x(t, dz, sub).start()
 
     @pl.when(layer == 0)
     def _():
         for t in range(steps):
             s_ref[t, unit] = emb_ref[t]
-            for dz in range(1, outer):
-                emb_z(t, dz).start()
-            emb_x(t, 0).start()
+            for sub in range(SUBS):
+                for dz in range(1, outer):
+                    emb_z(t, dz, sub).start()
+                emb_x(t, 0, sub).start()
 
     def w_copy(j):
         return pltpu.make_async_copy(w_hbm.at[j], w_ref.at[j], w_sem.at[j])
@@ -175,7 +183,7 @@
         carry_ref[q] = zero_tile
         cell_ref[0, q] = zero_tile
     for g in range(groups):
-        r_ref[g * (entries + 1) + entries] = zero_tile
+        r_ref[g * (entries + 1) + entries] = zero_tile.astype(BF16)
 
     @pl.when(layer == layers - 1)
     def _():
@@ -183,8 +191,9 @@
             for q in range(pairs):
                 d_ref[t, q] = jnp.zeros((rows, 128), BF16)
 
-    def unpack(src, t, v, base):
-        for q in range(pairs):
+    def unpack(src, t, v, base, sub):
+        for part_q in range(sub_pairs):
+            q = sub * sub_pairs + part_q
             tile = src[t, v, q].astype(F32)
             turned = swap(tile)
             at = base + v * own_blocks + 2 * q
@@ -197,35 +206,44 @@
 
     looped(own_blocks, 1, lambda j: w_copy(j).wait())
 
-    def own_copy_z(t, dz):
+    def own_copy_z(t, dz, sub):
+        here = part(h_ref, t, unit, sub)
         return remote(
-            h_ref.at[t, unit],
-            h_ref.at[t, unit],
-            z_send.at[dz],
-            h_recv.at[t, unit],
+            here,
+            here,
+            z_send.at[dz, sub],
+            h_recv.at[t, unit, sub],
             (layer, other_z(dz) * INNER + xpos),
         )
 
-    def copy_x(t, dz):
+    def copy_x(t, dz, sub):
         v = other_z(dz) * INNER + xpos
+        here = part(h_ref, t, v, sub)
+        return remote(here, here, x_send.at[dz, sub], h_recv.at[t, v, sub], (layer, partner))
+
+    def copy_up(t, v, sub):
         return remote(
-            h_ref.at[t, v], h_ref.at[t, v], x_send.at[dz], h_recv.at[t, v], (layer, partner)
+            part(h_ref, t, v, sub),
+            part(s_ref, t, v, sub),
+            up_send.at[v, sub],
+            s_recv.at[t, v, sub],
+            (layer + 1, unit),
         )
 
-    def copy_up(t, v):
-        return remote(
-            h_ref.at[t, v], s_ref.at[t, v], up_send.at[v], s_recv.at[t, v], (layer + 1, unit)
-        )
-
-    def h_wait(t, v):
+    def h_wait(t, v, sub):
+        here = part(h_ref, t, v, sub)
         remote(
-            h_ref.at[t, v], h_ref.at[t, v], x_send.at[0], h_recv.at[t, v], (layer, partner)
+            here, here, x_send.at[0, sub], h_recv.at[t, v, sub], (layer, partner)
         ).wait_recv()
 
     def wait_up(t):
         @pl.when((layers - 1 - layer) * (t + 1) > 0)
         def _():
-            looped(units, 1, lambda v: copy_up(t, v).wait_send())
+            def one(v):
+                for sub in range(SUBS):
+                    copy_up(t, v, sub).wait_send()
+
+            looped(units, 1, one)
 
     def forward(t, carry):
         def take_source(i):
@@ -233,9 +251,11 @@
 
             @pl.when(layer + lax.abs(lax.rem(v, INNER) - xpos) > 0)
             def _():
-                s_wait(t, v)
-
-            unpack(s_ref, t, v, 0)
+                for sub in range(SUBS):
+                    s_wait(t, v, sub)
+
+            for sub in range(SUBS):
+                unpack(s_ref, t, v, 0, sub)
 
         looped(units, 1, take_source)
 
@@ -249,7 +269,6 @@
                         jnp.where(low, x_ref[lay_ref[j, k]], x_ref[lay_ref[j, k + 1]])
                     )
                 picked = jnp.concatenate(tiles, axis=1)
-                g_ref[j, pl.ds(pl.multiple_of(t * rows, rows), rows), :] = picked
                 pres.append(
                     jnp.dot(picked, w_ref[j], preferred_element_type=F32)
                     + bias_ref[pl.ds(j, 1), :]
@@ -275,69 +294,96 @@
             h_ref[t, unit, q] = hidden
             hid_ref[t, :, pl.ds(pl.multiple_of(q * 128, 128), 128)] = hidden
 
-        looped(pairs, 2, cells)
-
         wait_up(t - 1)
+        for sub in range(SUBS):
+            looped(sub_pairs, 2, lambda i: cells(sub * sub_pairs + i))
+
+            @pl.when((layers - 1 - layer) + (steps - 1 - t) > 0)
+            def _():
+                for dz in range(1, outer):
+                    own_copy_z(t, dz, sub).start()
+                copy_x(t, 0, sub).start()
+
+                @pl.when(has_above)
+                def _():
+                    copy_up(t, unit, sub).start()
 
         @pl.when((layers - 1 - layer) + (steps - 1 - t) > 0)
         def _():
-            for dz in range(1, outer):
-                own_copy_z(t, dz).start()
-            copy_x(t, 0).start()
-
-            @pl.when(has_above)
-            def _():
-                copy_up(t, unit).start()
+            for sub in range(SUBS):
+                unpack(h_ref, t, unit, half_blocks, sub)
+
+            def arrived(dz, sub, is_partner):
+                v = other_z(dz) * INNER + (1 - xpos if is_partner else xpos)
+                h_wait(t, v, sub)
+                if not is_partner:
+                    copy_x(t, dz, sub).start()
+
+                @pl.when(has_above)
+                def _():
+                    copy_up(t, v, sub).start()
+
+                unpack(h_ref, t, v, half_blocks, sub)
+
+            for sub in range(SUBS):
+                looped(outer - 1, 1, lambda i: arrived(i + 1, sub, False))
 
             @pl.when(layer + lax.div(t + 1, steps) == 0)
             def _():
                 emb_forward(t + 1)
 
-            unpack(h_ref, t, unit, half_blocks)
-
-            def arrived(dz, is_partner):
-                v = other_z(dz) * INNER + (1 - xpos if is_partner else xpos)
-                h_wait(t, v)
-                if not is_partner:
-                    copy_x(t, dz).start()
-
-                @pl.when(has_above)
-                def _():
-                    copy_up(t, v).start()
-
-                unpack(h_ref, t, v, half_blocks)
-
-            looped(outer - 1, 1, lambda i: arrived(i + 1, False))
-            looped(outer, 1, lambda i: arrived(i, True))
-            for dz in range(1, outer):
-                own_copy_z(t, dz).wait_send()
-            for dz in range(outer):
-                copy_x(t, dz).wait_send()
+            for sub in range(SUBS):
+                looped(outer, 1, lambda i: arrived(i, sub, True))
+            for sub in range(SUBS):
+                for dz in range(1, outer):
+                    own_copy_z(t, dz, sub).wait_send()
+                for dz in range(outer):
+                    copy_x(t, dz, sub).wait_send()
 
         return carry
 
     lax.fori_loop(0, steps, forward, 0)
-    g_copy = pltpu.make_async_copy(g_ref, g_hbm, g_sem)
-    g_copy.start()
     wait_up(steps - 1)
 
+    xt_copy = pltpu.make_async_copy(xt_ref, xt_hbm, xt_sem)
+
+    def turn_inputs():
+        def one(at):
+            v = at // pairs
+            q = at % pairs
+            source = jnp.concatenate([s_ref[t, v, q] for t in range(steps)], axis=0).T
+            recur = jnp.concatenate(
+                [jnp.zeros((rows, 128), BF16)] + [h_ref[t, v, q] for t in range(steps - 1)],
+                axis=0,
+            ).T
+            for side in range(2):
+                xt_ref[2 * at + side] = source[side * 64 : side * 64 + 64]
+                xt_ref[half_blocks + 2 * at + side] = recur[side * 64 : side * 64 + 64]
+
+        looped(units * pairs, 2, one)
+        xt_copy.start()
+
+    @pl.when(has_above)
+    def _():
+        turn_inputs()
+
     @pl.when(layer == 0)
     def _():
         for t in range(steps):
-            for dz in range(1, outer):
-                emb_z(t, dz).wait_send()
-            for dz in range(outer):
-                emb_x(t, dz).wait_send()
+            for sub in range(SUBS):
+                for dz in range(1, outer):
+                    emb_z(t, dz, sub).wait_send()
+                for dz in range(outer):
+                    emb_x(t, dz, sub).wait_send()
 
     def group_sum(half, v, q):
         at = half * half_blocks + v * own_blocks + 2 * q
-        left = right = None
+        total = None
         for g in range(groups):
-            one = r_ref[last_ref[g, at]]
-            two = r_ref[last_ref[g, at + 1]]
-            left = one if left is None else left + one
-            right = two if right is None else right + two
-        return jnp.where(low, left, right)
+            both = jnp.where(low, r_ref[last_ref[g, at]], r_ref[last_ref[g, at + 1]])
+            both = both.astype(F32)
+            total = both if total is None else total + both
+        return total
 
     def copy_xr(t, half, z):
         return remote(
@@ -415,8 +461,8 @@
                     for k in range(0, nonzero, 2):
                         tile = contrib[:, k * 64 : k * 64 + 128]
                         turned = swap(tile)
-                        c_ref[jl * nonzero + k] = jnp.where(low, tile, turned)
-                        c_ref[jl * nonzero + k + 1] = jnp.where(low, turned, tile)
+                        c_ref[jl * nonzero + k] = jnp.where(low, tile, turned).astype(BF16)
+                        c_ref[jl * nonzero + k + 1] = jnp.where(low, turned, tile).astype(BF16)
 
                 looped(2 * per_group, 2, contributions)
 
@@ -426,11 +472,13 @@
                         r = r8 * 8 + part
                         for side in range(2):
                             g = gg * 2 + side
-                            run[side] = c_ref[perm_ref[g, r]] + same_ref[g, r] * run[side]
+                            keep = jnp.full((rows, 128), same_ref[g, r], F32).astype(BF16)
+                            run[side] = c_ref[perm_ref[g, r]] + keep * run[side]
                             r_ref[g * (entries + 1) + r] = run[side]
                     return tuple(run)
 
-                lax.fori_loop(0, entries // 8, runs, (zero_tile, zero_tile))
+                zero_run = zero_tile.astype(BF16)
+                lax.fori_loop(0, entries // 8, runs, (zero_run, zero_run))
                 return inner_carry
 
             lax.fori_loop(0, groups // 2, two_groups, 0)
@@ -503,15 +551,26 @@
         return carry
 
     lax.fori_loop(0, steps, backward, 0)
-    g_copy.wait()
-
-
-def weight_kernel(g_ref, gp_ref, gw_ref, gb_ref):
+
+    @pl.when(layer == layers - 1)
+    def _():
+        turn_inputs()
+
+    xt_copy.wait()
+
+
+def weight_kernel(lay_ref, xt_ref, gp_ref, hid_ref, gw_ref, gb_ref, out_ref):
+    j = pl.program_id(0)
     grad_pre = gp_ref[0]
-    gw_ref[0] = lax.dot_general(
-        g_ref[0], grad_pre, (((0,), (0,)), ((), ())), preferred_element_type=F32
-    ).astype(BF16)
-    gb_ref[0] = jnp.sum(grad_pre.astype(F32), axis=0, keepdims=True)
+    picked = jnp.concatenate(
+        [xt_ref[lay_ref[j, k]] for k in range(lay_ref.shape[1])], axis=0
+    )
+    gw_ref[0] = jnp.dot(picked, grad_pre, preferred_element_type=F32).astype(BF16)
+    gb_ref[pl.ds(j, 1), :] = jnp.sum(grad_pre.astype(F32), axis=0, keepdims=True)
+
+    @pl.when(j == 0)
+    def _():
+        out_ref[...] = hid_ref[...]
 
 
 def on_device(layers, units, tokens, embed, weights, layout, bias, d_hidden):
@@ -552,25 +611,25 @@
     hbm = pl.BlockSpec(memory_space=pl.ANY)
     tile = (rows, 128)
     dma = pltpu.SemaphoreType.DMA
-    hidden, picked, grad_pre = pl.pallas_call(
+    hidden, inputs_t, grad_pre = pl.pallas_call(
         functools.partial(lstm_kernel, layers, units, groups),
         out_shape=(
             jax.ShapeDtypeStruct((steps, rows, width), BF16),
-            jax.ShapeDtypeStruct((own_blocks, steps * rows, depth), BF16),
+            jax.ShapeDtypeStruct((2 * half_blocks, block, steps * rows), BF16),
             jax.ShapeDtypeStruct((own_blocks, steps * rows, gates), BF16),
         ),
         in_specs=[smem, smem, smem, smem, vmem, hbm, vmem, vmem],
         out_specs=(vmem, hbm, vmem),
         scratch_shapes=[
             pltpu.VMEM((own_blocks, depth, gates), BF16),
-            pltpu.VMEM((own_blocks, steps * rows, depth), BF16),
+            pltpu.VMEM((2 * half_blocks, block, steps * rows), BF16),
             pltpu.VMEM((2 * half_blocks,) + tile, BF16),
             pltpu.VMEM((steps, units, pairs) + tile, BF16),
             pltpu.VMEM((steps, units, pairs) + tile, BF16),
             pltpu.VMEM((5, steps, pairs) + tile, F32),
             pltpu.VMEM((steps + 1, pairs) + tile, F32),
-            pltpu.VMEM((2 * entries,) + tile, F32),
-            pltpu.VMEM((groups * (entries + 1),) + tile, F32),
+            pltpu.VMEM((2 * entries,) + tile, BF16),
+            pltpu.VMEM((groups * (entries + 1),) + tile, BF16),
             pltpu.VMEM((2, outer, pairs) + tile, BF16),
             pltpu.VMEM((steps, 2, outer, pairs) + tile, BF16),
             pltpu.VMEM((steps, 2, outer, pairs) + tile, BF16),
@@ -581,13 +640,13 @@
             pltpu.VMEM((pairs,) + tile, F32),
             dma((own_blocks,)),
             dma,
-            dma((steps, units)),
-            dma((steps, units)),
-            dma((outer,)),
-            dma((outer,)),
-            dma((units,)),
-            dma((steps, outer)),
-            dma((steps, outer)),
+            dma((steps, units, SUBS)),
+            dma((steps, units, SUBS)),
+            dma((outer, SUBS)),
+            dma((outer, SUBS)),
+            dma((units, SUBS)),
+            dma((steps, outer, SUBS)),
+            dma((steps, outer, SUBS)),
             dma((steps, 2, outer)),
             dma((steps, 2, outer)),
             dma((2, outer)),
@@ -601,27 +660,33 @@
         name="lstm",
     )(lay, perm, same, last, emb, weights[0].reshape(own_blocks, depth, gates), bias[0], d_hidden[0])
 
-    grad_w, grad_b = pl.pallas_call(
+    whole = lambda shape: pl.BlockSpec(shape, lambda j: (0,) * len(shape))
+    grad_w, grad_b, hidden = pl.pallas_call(
         weight_kernel,
         grid=(own_blocks,),
         out_shape=(
             jax.ShapeDtypeStruct((own_blocks, depth, gates), BF16),
-            jax.ShapeDtypeStruct((own_blocks, 1, gates), F32),
+            jax.ShapeDtypeStruct((own_blocks, gates), F32),
+            jax.ShapeDtypeStruct((steps, rows, width), BF16),
         ),
         in_specs=[
-            pl.BlockSpec((1, steps * rows, depth), lambda j: (j, 0, 0)),
+            smem,
+            whole((2 * half_blocks, block, steps * rows)),
             pl.BlockSpec((1, steps * rows, gates), lambda j: (j, 0, 0)),
+            whole((steps, rows, width)),
         ],
         out_specs=(
             pl.BlockSpec((1, depth, gates), lambda j: (j, 0, 0)),
-            pl.BlockSpec((1, 1, gates), lambda j: (j, 0, 0)),
+            whole((own_blocks, gates)),
+            whole((steps, rows, width)),
         ),
+        compiler_params=pltpu.CompilerParams(vmem_limit_bytes=32 * 2**20),
         name="grad_weights",
-    )(picked, grad_pre)
+    )(lay, inputs_t, grad_pre, hidden)
     return (
         hidden[None],
         grad_w.reshape(1, own_blocks, nonzero, block, gates),
-        grad_b.reshape(1, own_blocks, gates),
+        grad_b[None],
     )
 
 

time: 288 us -> 268 us (0.931)
  Pallas kernels: 278 us -> 257 us
    pallas_call x1, Pallas kernels: 261 us -> 245 us  [on_device(): pl.pallas_call(functools.partial(lstm_kernel, layers, units, groups), out...]
    pallas_call x1, Pallas kernels: 16.6 us -> 12.3 us  [on_device(): pl.pallas_call(weight_kernel, grid=(own_blocks,), out_shape=(jax.ShapeDty...]
where the time goes in v2:
time: 268 us
  Pallas kernels  257 us (96%)
  local copies, waits for them, and re-layouts  6.75 us (3%)
  other arithmetic  2.98 us (1%)
    pallas_call x1, Pallas kernels, on_device(): pl.pallas_call(functools.partial(lstm_kernel, layers, units, groups), out...  245 us
    pallas_call x1, Pallas kernels, on_device(): pl.pallas_call(weight_kernel, grid=(own_blocks,), out_shape=(jax.ShapeDty...  12.3 us

profile of v2, /device:TPU:0, one launch (start us, length us, event | category | flops | bytes accessed | tf_op | source)
XLA Modules:
  0.0 267.9 jit_solution(1370644254477854669)
XLA Ops:
  0.6 0.0 copy-start
  0.6 0.0 copy-start.4
  0.7 0.8 eq.56
  1.5 0.8 reshape_squeeze.6
  2.3 0.2 fusion.1
  2.5 0.2 convert_reduce_fusion.1
  2.7 0.2 select_reduce_fusion
  3.0 0.1 slice_compare_fusion
  3.0 0.7 pad_convert_fusion.same_ref
  3.7 0.6 broadcast_add_fusion.perm_ref
  4.4 0.2 convert_reduce_fusion
  4.6 0.7 select_add_fusion.last_ref
  5.2 0.0 copy-done
  5.2 0.3 fusion
  5.6 0.7 copy.13
  6.3 244.9 %lstm.1 = (bf16[4,32,1024]{2,1,0:T(8,128)(2,1)}, bf16[256,64,128]{2,1,0:T(8,128)(2,1)}, bf16[16,128,256]{2,1,0:T(8,128)(2,1)}) custom-call(s32[16,32]{1,0:T(8,128)} %bitcast.15, s32[4,128]{1,0:T(4,128)} %broadcast_add_fusion.perm_ref, f32[4,128]{1,0:T(4,128)} %pad_convert_fusion.same_ref, s32[4,256]{1,0:T(4,128)} %select_add_fusion.last_ref, ...), custom_call_target="tpu_custom_call" | custom-call | tf_op jit(solution)/shard_map/lstm/pallas_call | solution.py:614
  251.2 0.0 copy-done.4
  251.2 0.0 copy-start.1
  251.2 2.2 copy-done.1
  253.4 0.0 copy-start.2
  253.4 1.2 copy-done.2
  254.6 0.0 copy-start.3
  254.6 0.9 copy-done.3
  255.6 12.3 %grad_weights.1 = (bf16[16,2048,256]{2,1,0:T(8,128)(2,1)}, f32[16,256]{1,0:T(8,128)}, bf16[4,32,1024]{2,1,0:T(8,128)(2,1)}) custom-call(s32[16,32]{1,0:T(8,128)S(1)} %bitcast.16, bf16[256,64,128]{2,1,0:T(8,128)(2,1)S(1)} %copy-done.1, bf16[16,128,256]{2,1,0:T(8,128)(2,1)S(1)} %copy-done.2, bf16[4,32,1024]{2,1,0:T(8,128)(2,1)S(1)} %copy-done.3), custom_call_target="tpu_custom_call" | custom-call | tf_op jit(solution)/shard_map/grad_weights/pallas_call | solution.py:664
  (4 shorter events, 0.1 us)
Async XLA Ops:
  0.6 4.6 %copy-start = (bf16[256,1024]{1,0:T(8,128)(2,1)S(1)}, bf16[256,1024]{1,0:T(8,128)(2,1)}, u32[]{:S(2)}) copy-start(bf16[256,1024]{1,0:T(8,128)(2,1)} %param.7) | copy-start | bytes 1572868
  0.6 250.6 %copy-start.4 = (s32[1,16,32]{2,1,0:T(8,128)S(1)}, s32[1,16,32]{2,1,0:T(8,128)}, u32[]{:S(2)}) copy-start(s32[1,16,32]{2,1,0:T(8,128)} %param.9) | copy-start | bytes 6148
  251.2 2.2 copy-start.1
  253.4 1.2 copy-start.2
  254.6 0.9 copy-start.3

commit v3 on v2

--- a/solution.py
+++ b/solution.py
@@ -42,6 +42,7 @@
     xt_hbm,
     gp_ref,
     w_ref,
+    wt_ref,
     xt_ref,
     x_ref,
     h_ref,
@@ -86,7 +87,6 @@
     sub_pairs = pairs // SUBS
     half_blocks = units * own_blocks
     entries = own_blocks * nonzero // groups
-    per_group = own_blocks // groups
     has_above = layer < layers - 1
     has_below = layer > 0
     low = lax.broadcasted_iota(jnp.int32, (rows, 128), 1) < 64
@@ -205,6 +205,19 @@
         emb_forward(0)
 
     looped(own_blocks, 1, lambda j: w_copy(j).wait())
+
+    def turn_weights():
+        depth, gates = w_ref.shape[1:]
+
+        def one(j):
+            for at in range(0, depth, gates):
+                wt_ref[j, :, at : at + gates] = w_ref[j, at : at + gates, :].T
+
+        looped(own_blocks, 1, one)
+
+    @pl.when(layer >= layers // 2)
+    def _():
+        turn_weights()
 
     def own_copy_z(t, dz, sub):
         here = part(h_ref, t, unit, sub)
@@ -347,6 +360,10 @@
 
     xt_copy = pltpu.make_async_copy(xt_ref, xt_hbm, xt_sem)
 
+    @pl.when(layer < layers // 2)
+    def _():
+        turn_weights()
+
     def turn_inputs():
         def one(at):
             v = at // pairs
@@ -451,37 +468,30 @@
 
         @pl.when(layer + t > 0)
         def _():
-            def two_groups(gg, inner_carry):
-                def contributions(jl):
-                    j = gg * (2 * per_group) + jl
-                    grad_pre = gp_ref[j, pl.ds(pl.multiple_of(t * rows, rows), rows), :]
-                    contrib = lax.dot_general(
-                        grad_pre, w_ref[j], (((1,), (1,)), ((), ())), preferred_element_type=F32
-                    )
-                    for k in range(0, nonzero, 2):
-                        tile = contrib[:, k * 64 : k * 64 + 128]
-                        turned = swap(tile)
-                        c_ref[jl * nonzero + k] = jnp.where(low, tile, turned).astype(BF16)
-                        c_ref[jl * nonzero + k + 1] = jnp.where(low, turned, tile).astype(BF16)
-
-                looped(2 * per_group, 2, contributions)
-
-                def runs(r8, run):
-                    run = list(run)
-                    for part in range(8):
-                        r = r8 * 8 + part
-                        for side in range(2):
-                            g = gg * 2 + side
-                            keep = jnp.full((rows, 128), same_ref[g, r], F32).astype(BF16)
-                            run[side] = c_ref[perm_ref[g, r]] + keep * run[side]
-                            r_ref[g * (entries + 1) + r] = run[side]
-                    return tuple(run)
-
-                zero_run = zero_tile.astype(BF16)
-                lax.fori_loop(0, entries // 8, runs, (zero_run, zero_run))
-                return inner_carry
-
-            lax.fori_loop(0, groups // 2, two_groups, 0)
+            def contributions(j):
+                grad_pre = gp_ref[j, pl.ds(pl.multiple_of(t * rows, rows), rows), :]
+                contrib = jnp.dot(grad_pre, wt_ref[j], preferred_element_type=F32)
+                for k in range(0, nonzero, 2):
+                    tile = contrib[:, k * 64 : k * 64 + 128]
+                    turned = swap(tile)
+                    at = j * nonzero + k
+                    c_ref[at] = jnp.where(low, tile, turned).astype(BF16)
+                    c_ref[at + 1] = jnp.where(low, turned, tile).astype(BF16)
+
+            looped(own_blocks, 2, contributions)
+
+            def runs(r8, run):
+                run = list(run)
+                for part_r in range(8):
+                    r = r8 * 8 + part_r
+                    for g in range(groups):
+                        keep = jnp.full((rows, 128), same_ref[g, r], F32).astype(BF16)
+                        run[g] = c_ref[perm_ref[g, r]] + keep * run[g]
+                        r_ref[g * (entries + 1) + r] = run[g]
+                return tuple(run)
+
+            zero_run = zero_tile.astype(BF16)
+            lax.fori_loop(0, entries // 8, runs, (zero_run,) * groups)
 
             def per_half(do):
                 @pl.when(t > 0)
@@ -600,7 +610,7 @@
         [jnp.zeros((groups, 1), F32), (ordered[:, 1:] == ordered[:, :-1]).astype(F32)], 1
     )
     group_ids = jnp.arange(groups, dtype=jnp.int32)[:, None]
-    perm = perm + (group_ids % 2) * entries
+    perm = perm + group_ids * entries
     blocks = jnp.arange(2 * half_blocks, dtype=jnp.int32)[:, None]
     below = jnp.sum((ent[:, None, :] <= blocks).astype(jnp.int32), -1)
     present = jnp.any(ent[:, None, :] == blocks, -1)
@@ -622,13 +632,14 @@
         out_specs=(vmem, hbm, vmem),
         scratch_shapes=[
             pltpu.VMEM((own_blocks, depth, gates), BF16),
+            pltpu.VMEM((own_blocks, gates, depth), BF16),
             pltpu.VMEM((2 * half_blocks, block, steps * rows), BF16),
             pltpu.VMEM((2 * half_blocks,) + tile, BF16),
             pltpu.VMEM((steps, units, pairs) + tile, BF16),
             pltpu.VMEM((steps, units, pairs) + tile, BF16),
             pltpu.VMEM((5, steps, pairs) + tile, F32),
             pltpu.VMEM((steps + 1, pairs) + tile, F32),
-            pltpu.VMEM((2 * entries,) + tile, BF16),
+            pltpu.VMEM((groups * entries,) + tile, BF16),
             pltpu.VMEM((groups * (entries + 1),) + tile, BF16),
             pltpu.VMEM((2, outer, pairs) + tile, BF16),
             pltpu.VMEM((steps, 2, outer, pairs) + tile, BF16),
@@ -655,7 +666,7 @@
             dma,
         ],
         compiler_params=pltpu.CompilerParams(
-            collective_id=0, has_side_effects=True, vmem_limit_bytes=60 * 2**20
+            collective_id=0, has_side_effects=True, vmem_limit_bytes=62 * 2**20
         ),
         name="lstm",
     )(lay, perm, same, last, emb, weights[0].reshape(own_blocks, depth, gates), bias[0], d_hidden[0])

time: 268 us -> 254 us (0.948)
  Pallas kernels: 257 us -> 243 us
    pallas_call x1, Pallas kernels: 245 us -> 231 us  [on_device(): pl.pallas_call(functools.partial(lstm_kernel, layers, units, groups), out...]
where the time goes in v3:
time: 254 us
  Pallas kernels  243 us (96%)
  local copies, waits for them, and re-layouts  6.75 us (3%)
  other arithmetic  2.98 us (1%)
    pallas_call x1, Pallas kernels, on_device(): pl.pallas_call(functools.partial(lstm_kernel, layers, units, groups), out...  231 us
    pallas_call x1, Pallas kernels, on_device(): pl.pallas_call(weight_kernel, grid=(own_blocks,), out_shape=(jax.ShapeDty...  12.3 us

profile of v3, /device:TPU:0, one launch (start us, length us, event | category | flops | bytes accessed | tf_op | source)
XLA Modules:
  0.0 253.6 jit_solution(11298026561400634485)
XLA Ops:
  0.6 0.0 copy-start
  0.6 0.0 copy-start.4
  0.7 0.8 eq.54
  1.5 0.8 reshape_squeeze.6
  2.3 0.2 fusion.1
  2.5 0.2 convert_reduce_fusion.1
  2.7 0.2 select_reduce_fusion
  3.0 0.1 slice_compare_fusion
  3.0 0.7 pad_convert_fusion.same_ref
  3.7 0.6 broadcast_add_fusion.perm_ref
  4.4 0.2 convert_reduce_fusion
  4.6 0.7 select_add_fusion.last_ref
  5.2 0.0 copy-done
  5.2 0.3 fusion
  5.6 0.7 copy.13
  6.3 230.6 %lstm.1 = (bf16[4,32,1024]{2,1,0:T(8,128)(2,1)}, bf16[256,64,128]{2,1,0:T(8,128)(2,1)}, bf16[16,128,256]{2,1,0:T(8,128)(2,1)}) custom-call(s32[16,32]{1,0:T(8,128)} %bitcast.15, s32[4,128]{1,0:T(4,128)} %broadcast_add_fusion.perm_ref, f32[4,128]{1,0:T(4,128)} %pad_convert_fusion.same_ref, s32[4,256]{1,0:T(4,128)} %select_add_fusion.last_ref, ...), custom_call_target="tpu_custom_call" | custom-call | tf_op jit(solution)/shard_map/lstm/pallas_call | solution.py:624
  236.9 0.0 copy-done.4
  236.9 0.0 copy-start.1
  236.9 2.2 copy-done.1
  239.1 0.0 copy-start.2
  239.1 1.2 copy-done.2
  240.3 0.0 copy-start.3
  240.3 0.9 copy-done.3
  241.3 12.3 %grad_weights.1 = (bf16[16,2048,256]{2,1,0:T(8,128)(2,1)}, f32[16,256]{1,0:T(8,128)}, bf16[4,32,1024]{2,1,0:T(8,128)(2,1)}) custom-call(s32[16,32]{1,0:T(8,128)S(1)} %bitcast.16, bf16[256,64,128]{2,1,0:T(8,128)(2,1)S(1)} %copy-done.1, bf16[16,128,256]{2,1,0:T(8,128)(2,1)S(1)} %copy-done.2, bf16[4,32,1024]{2,1,0:T(8,128)(2,1)S(1)} %copy-done.3), custom_call_target="tpu_custom_call" | custom-call | tf_op jit(solution)/shard_map/grad_weights/pallas_call | solution.py:675
  (4 shorter events, 0.1 us)
Async XLA Ops:
  0.6 4.6 %copy-start = (bf16[256,1024]{1,0:T(8,128)(2,1)S(1)}, bf16[256,1024]{1,0:T(8,128)(2,1)}, u32[]{:S(2)}) copy-start(bf16[256,1024]{1,0:T(8,128)(2,1)} %param.7) | copy-start | bytes 1572868
  0.6 236.3 %copy-start.4 = (s32[1,16,32]{2,1,0:T(8,128)S(1)}, s32[1,16,32]{2,1,0:T(8,128)}, u32[]{:S(2)}) copy-start(s32[1,16,32]{2,1,0:T(8,128)} %param.9) | copy-start | bytes 6148
  236.9 2.2 copy-start.1
  239.1 1.2 copy-start.2
  240.3 0.9 copy-start.3

commit v4 on v3

--- a/solution.py
+++ b/solution.py
@@ -402,44 +402,74 @@
             total = both if total is None else total + both
         return total
 
-    def copy_xr(t, half, z):
+    def cut(ref, *at):
+        *front, sub = at
+        return ref.at[(*front, pl.ds(sub * sub_pairs, sub_pairs))]
+
+    def copy_xr(t, half, z, sub):
         return remote(
-            p_ref.at[half, z],
-            xr_ref.at[t, half, z],
-            xr_send.at[half, z],
-            xr_recv.at[t, half, z],
+            cut(p_ref, half, z, sub),
+            cut(xr_ref, t, half, z, sub),
+            xr_send.at[half, z, sub],
+            xr_recv.at[t, half, z, sub],
             (layer, partner),
         )
 
-    def copy_zr(t, half, dz):
+    def copy_zr(t, half, dz, sub):
         z = other_z(dz)
         return remote(
-            q_ref.at[half, z],
-            zr_ref.at[t, half, zpos],
-            zr_send.at[half, z],
-            zr_recv.at[t, half, zpos],
+            cut(q_ref, half, z, sub),
+            cut(zr_ref, t, half, zpos, sub),
+            zr_send.at[half, z, sub],
+            zr_recv.at[t, half, zpos, sub],
             (layer, z * INNER + xpos),
         )
 
-    def wait_zr(t, half, dz):
+    def wait_zr(t, half, dz, sub):
         z = other_z(dz)
         remote(
-            q_ref.at[half, z],
-            zr_ref.at[t, half, z],
-            zr_send.at[half, z],
-            zr_recv.at[t, half, z],
+            cut(q_ref, half, z, sub),
+            cut(zr_ref, t, half, z, sub),
+            zr_send.at[half, z, sub],
+            zr_recv.at[t, half, z, sub],
             (layer, z * INNER + xpos),
         ).wait_recv()
 
-    def copy_down(t):
-        return remote(ds_ref, d_ref.at[t], d_send, d_recv.at[t], (layer - 1, unit))
+    def copy_down(t, sub, where_to):
+        return remote(
+            cut(ds_ref, sub), cut(d_ref, t, sub), d_send.at[sub], d_recv.at[t, sub], where_to
+        )
+
+    def finish(t, half, sub):
+        copy_xr(t, half, zpos, sub).wait_recv()
+        for dz in range(1, outer):
+            wait_zr(t, half, dz, sub)
+
+        def one(i):
+            q = sub * sub_pairs + i
+            total = group_sum(half, unit, q) + xr_ref[t, half, zpos, q].astype(F32)
+            for dz in range(1, outer):
+                total = total + zr_ref[t, half, other_z(dz), q].astype(F32)
+            if half:
+                rec_ref[q] = total
+            else:
+                ds_ref[q] = total.astype(BF16)
+
+        looped(sub_pairs, 4, one)
+        if not half:
+            copy_down(t, sub, (layer - 1, unit)).start()
+
+    def settle(t, half):
+        for sub in range(SUBS):
+            for z in range(outer):
+                copy_xr(t, half, z, sub).wait_send()
+            for dz in range(1, outer):
+                copy_zr(t, half, dz, sub).wait_send()
+            if not half:
+                copy_down(t, sub, (layer - 1, unit)).wait_send()
 
     def backward(i, carry):
         t = steps - 1 - i
-
-        @pl.when(has_above)
-        def _():
-            remote(ds_ref, d_ref.at[t], d_send, d_recv.at[t], (layer + 1, unit)).wait_recv()
 
         def cells(q):
             grad_hidden = (
@@ -464,22 +494,46 @@
             gp_ref[2 * q + 1, at, :128] = jnp.where(low, swap(gi), gf).astype(BF16)
             gp_ref[2 * q + 1, at, 128:] = jnp.where(low, swap(gu), go).astype(BF16)
 
-        looped(pairs, 2, cells)
+        def contributions(j):
+            grad_pre = gp_ref[j, pl.ds(pl.multiple_of(t * rows, rows), rows), :]
+            contrib = jnp.dot(grad_pre, wt_ref[j], preferred_element_type=F32)
+            for k in range(0, nonzero, 2):
+                tile = contrib[:, k * 64 : k * 64 + 128]
+                turned = swap(tile)
+                at = j * nonzero + k
+                c_ref[at] = jnp.where(low, tile, turned).astype(BF16)
+                c_ref[at + 1] = jnp.where(low, turned, tile).astype(BF16)
+
+        for sub in range(SUBS):
+
+            @pl.when(i > 0)
+            def _():
+                finish(t + 1, 1, sub)
+
+                @pl.when(has_below)
+                def _():
+                    finish(t + 1, 0, sub)
+
+            @pl.when(has_above)
+            def _():
+                copy_down(t, sub, (layer + 1, unit)).wait_recv()
+
+            looped(sub_pairs, 4, lambda part_q: cells(sub * sub_pairs + part_q))
+
+            @pl.when(layer + t > 0)
+            def _():
+                looped(2 * sub_pairs, 2, lambda part_j: contributions(2 * sub * sub_pairs + part_j))
+
+        @pl.when(i > 0)
+        def _():
+            settle(t + 1, 1)
+
+            @pl.when(has_below)
+            def _():
+                settle(t + 1, 0)
 
         @pl.when(layer + t > 0)
         def _():
-            def contributions(j):
-                grad_pre = gp_ref[j, pl.ds(pl.multiple_of(t * rows, rows), rows), :]
-                contrib = jnp.dot(grad_pre, wt_ref[j], preferred_element_type=F32)
-                for k in range(0, nonzero, 2):
-                    tile = contrib[:, k * 64 : k * 64 + 128]
-                    turned = swap(tile)
-                    at = j * nonzero + k
-                    c_ref[at] = jnp.where(low, tile, turned).astype(BF16)
-                    c_ref[at + 1] = jnp.where(low, turned, tile).astype(BF16)
-
-            looped(own_blocks, 2, contributions)
-
             def runs(r8, run):
                 run = list(run)
                 for part_r in range(8):
@@ -502,66 +556,48 @@
                 def _():
                     do(0)
 
-            def send_partner(half):
-                def one(i):
-                    z = other_z(lax.rem(i + 1, outer))
-                    for q in range(pairs):
+            def send_partner(half, sub):
+                def one(step):
+                    z = other_z(lax.rem(step + 1, outer))
+                    for part_q in range(sub_pairs):
+                        q = sub * sub_pairs + part_q
                         p_ref[half, z, q] = group_sum(
                             half, z * INNER + (1 - xpos), q
                         ).astype(BF16)
-                    copy_xr(t, half, z).start()
+                    copy_xr(t, half, z, sub).start()
 
                 looped(outer, 1, one)
 
-            def send_along(half):
-                def one(i):
-                    dz = i + 1
+            def send_along(half, sub):
+                def one(step):
+                    dz = step + 1
                     z = other_z(dz)
-                    copy_xr(t, half, z).wait_recv()
-                    for q in range(pairs):
+                    copy_xr(t, half, z, sub).wait_recv()
+                    for part_q in range(sub_pairs):
+                        q = sub * sub_pairs + part_q
                         q_ref[half, z, q] = (
                             group_sum(half, z * INNER + xpos, q)
                             + xr_ref[t, half, z, q].astype(F32)
                         ).astype(BF16)
-                    copy_zr(t, half, dz).start()
+                    copy_zr(t, half, dz, sub).start()
 
                 looped(outer - 1, 1, one)
 
-            def finish(half):
-                copy_xr(t, half, zpos).wait_recv()
-                for dz in range(1, outer):
-                    wait_zr(t, half, dz)
-
-                def one(q):
-                    total = group_sum(half, unit, q) + xr_ref[t, half, zpos, q].astype(F32)
-                    for dz in range(1, outer):
-                        total = total + zr_ref[t, half, other_z(dz), q].astype(F32)
-                    if half:
-                        rec_ref[q] = total
-                    else:
-                        ds_ref[q] = total.astype(BF16)
-
-                looped(pairs, 2, one)
-                if not half:
-                    copy_down(t).start()
-
-            def settle(half):
-                for z in range(outer):
-                    copy_xr(t, half, z).wait_send()
-                for dz in range(1, outer):
-                    copy_zr(t, half, dz).wait_send()
-                if not half:
-                    copy_down(t).wait_send()
-
-            per_half(send_partner)
-            per_half(send_along)
-            per_half(finish)
-            per_half(settle)
+            for sub in range(SUBS):
+                per_half(lambda half: send_partner(half, sub))
+            for sub in range(SUBS):
+                per_half(lambda half: send_along(half, sub))
 
         return carry
 
     lax.fori_loop(0, steps, backward, 0)
 
+    @pl.when(has_below)
+    def _():
+        for sub in range(SUBS):
+            finish(0, 0, sub)
+        settle(0, 0)
+
     @pl.when(layer == layers - 1)
     def _():
         turn_inputs()
@@ -570,15 +606,17 @@
 
 
 def weight_kernel(lay_ref, xt_ref, gp_ref, hid_ref, gw_ref, gb_ref, out_ref):
-    j = pl.program_id(0)
-    grad_pre = gp_ref[0]
-    picked = jnp.concatenate(
-        [xt_ref[lay_ref[j, k]] for k in range(lay_ref.shape[1])], axis=0
-    )
-    gw_ref[0] = jnp.dot(picked, grad_pre, preferred_element_type=F32).astype(BF16)
-    gb_ref[pl.ds(j, 1), :] = jnp.sum(grad_pre.astype(F32), axis=0, keepdims=True)
-
-    @pl.when(j == 0)
+    step = pl.program_id(0)
+    for part in range(gp_ref.shape[0]):
+        j = step * gp_ref.shape[0] + part
+        grad_pre = gp_ref[part]
+        picked = jnp.concatenate(
+            [xt_ref[lay_ref[j, k]] for k in range(lay_ref.shape[1])], axis=0
+        )
+        gw_ref[part] = jnp.dot(picked, grad_pre, preferred_element_type=F32).astype(BF16)
+        gb_ref[pl.ds(j, 1), :] = jnp.sum(grad_pre.astype(F32), axis=0, keepdims=True)
+
+    @pl.when(step == 0)
     def _():
         out_ref[...] = hid_ref[...]
 
@@ -658,12 +696,12 @@
             dma((units, SUBS)),
             dma((steps, outer, SUBS)),
             dma((steps, outer, SUBS)),
-            dma((steps, 2, outer)),
-            dma((steps, 2, outer)),
-            dma((2, outer)),
-            dma((2, outer)),
-            dma((steps,)),
-            dma,
+            dma((steps, 2, outer, SUBS)),
+            dma((steps, 2, outer, SUBS)),
+            dma((2, outer, SUBS)),
+            dma((2, outer, SUBS)),
+            dma((steps, SUBS)),
+            dma((SUBS,)),
         ],
         compiler_params=pltpu.CompilerParams(
             collective_id=0, has_side_effects=True, vmem_limit_bytes=62 * 2**20
@@ -674,7 +712,7 @@
     whole = lambda shape: pl.BlockSpec(shape, lambda j: (0,) * len(shape))
     grad_w, grad_b, hidden = pl.pallas_call(
         weight_kernel,
-        grid=(own_blocks,),
+        grid=(own_blocks // 2,),
         out_shape=(
             jax.ShapeDtypeStruct((own_blocks, depth, gates), BF16),
             jax.ShapeDtypeStruct((own_blocks, gates), F32),
@@ -683,11 +721,11 @@
         in_specs=[
             smem,
             whole((2 * half_blocks, block, steps * rows)),
-            pl.BlockSpec((1, steps * rows, gates), lambda j: (j, 0, 0)),
+            pl.BlockSpec((2, steps * rows, gates), lambda j: (j, 0, 0)),
             whole((steps, rows, width)),
         ],
         out_specs=(
-            pl.BlockSpec((1, depth, gates), lambda j: (j, 0, 0)),
+            pl.BlockSpec((2, depth, gates), lambda j: (j, 0, 0)),
             whole((own_blocks, gates)),
             whole((steps, rows, width)),
         ),

time: 254 us -> 234 us (0.921)
  Pallas kernels: 243 us -> 223 us
    pallas_call x1, Pallas kernels: 231 us -> 214 us  [on_device(): pl.pallas_call(functools.partial(lstm_kernel, layers, units, groups), out...]
    pallas_call x1, Pallas kernels: 12.3 us -> 9.51 us  [on_device(): pl.pallas_call(weight_kernel, grid=(own_blocks // 2,), out_shape=(jax.Sha...]
where the time goes in v4:
time: 234 us
  Pallas kernels  223 us (95%)
  local copies, waits for them, and re-layouts  6.75 us (3%)
  other arithmetic  2.98 us (1%)
    pallas_call x1, Pallas kernels, on_device(): pl.pallas_call(functools.partial(lstm_kernel, layers, units, groups), out...  214 us
    pallas_call x1, Pallas kernels, on_device(): pl.pallas_call(weight_kernel, grid=(own_blocks // 2,), out_shape=(jax.Sha...  9.51 us

profile of v4, /device:TPU:0, one launch (start us, length us, event | category | flops | bytes accessed | tf_op | source)
XLA Modules:
  0.0 234.0 jit_solution(9558724332574203009)
XLA Ops:
  0.6 0.0 copy-start
  0.6 0.0 copy-start.4
  0.7 0.8 eq.54
  1.5 0.8 reshape_squeeze.6
  2.3 0.2 fusion.1
  2.5 0.2 convert_reduce_fusion.1
  2.7 0.2 select_reduce_fusion
  3.0 0.1 slice_compare_fusion
  3.0 0.7 pad_convert_fusion.same_ref
  3.7 0.6 broadcast_add_fusion.perm_ref
  4.4 0.2 convert_reduce_fusion
  4.6 0.7 select_add_fusion.last_ref
  5.2 0.0 copy-done
  5.2 0.3 fusion
  5.6 0.7 copy.13
  6.3 213.8 %lstm.1 = (bf16[4,32,1024]{2,1,0:T(8,128)(2,1)}, bf16[256,64,128]{2,1,0:T(8,128)(2,1)}, bf16[16,128,256]{2,1,0:T(8,128)(2,1)}) custom-call(s32[16,32]{1,0:T(8,128)} %bitcast.15, s32[4,128]{1,0:T(4,128)} %broadcast_add_fusion.perm_ref, f32[4,128]{1,0:T(4,128)} %pad_convert_fusion.same_ref, s32[4,256]{1,0:T(4,128)} %select_add_fusion.last_ref, ...), custom_call_target="tpu_custom_call" | custom-call | tf_op jit(solution)/shard_map/lstm/pallas_call | solution.py:662
  220.2 0.0 copy-done.4
  220.2 0.0 copy-start.1
  220.2 2.2 copy-done.1
  222.3 0.0 copy-start.2
  222.4 1.2 copy-done.2
  223.6 0.0 copy-start.3
  223.6 0.9 copy-done.3
  224.5 9.5 %grad_weights.1 = (bf16[16,2048,256]{2,1,0:T(8,128)(2,1)}, f32[16,256]{1,0:T(8,128)}, bf16[4,32,1024]{2,1,0:T(8,128)(2,1)}) custom-call(s32[16,32]{1,0:T(8,128)S(1)} %bitcast.16, bf16[256,64,128]{2,1,0:T(8,128)(2,1)S(1)} %copy-done.1, bf16[16,128,256]{2,1,0:T(8,128)(2,1)S(1)} %copy-done.2, bf16[4,32,1024]{2,1,0:T(8,128)(2,1)S(1)} %copy-done.3), custom_call_target="tpu_custom_call" | custom-call | tf_op jit(solution)/shard_map/grad_weights/pallas_call | solution.py:713
  (4 shorter events, 0.1 us)
Async XLA Ops:
  0.6 4.6 %copy-start = (bf16[256,1024]{1,0:T(8,128)(2,1)S(1)}, bf16[256,1024]{1,0:T(8,128)(2,1)}, u32[]{:S(2)}) copy-start(bf16[256,1024]{1,0:T(8,128)(2,1)} %param.7) | copy-start | bytes 1572868
  0.6 219.5 %copy-start.4 = (s32[1,16,32]{2,1,0:T(8,128)S(1)}, s32[1,16,32]{2,1,0:T(8,128)}, u32[]{:S(2)}) copy-start(s32[1,16,32]{2,1,0:T(8,128)} %param.9) | copy-start | bytes 6148
  220.2 2.2 copy-start.1
  222.3 1.2 copy-start.2
  223.6 0.9 copy-start.3

commit v5 on v4

--- a/solution.py
+++ b/solution.py
@@ -309,7 +309,7 @@
 
         wait_up(t - 1)
         for sub in range(SUBS):
-            looped(sub_pairs, 2, lambda i: cells(sub * sub_pairs + i))
+            looped(sub_pairs, 4, lambda i: cells(sub * sub_pairs + i))
 
             @pl.when((layers - 1 - layer) + (steps - 1 - t) > 0)
             def _():
@@ -522,7 +522,7 @@
 
             @pl.when(layer + t > 0)
             def _():
-                looped(2 * sub_pairs, 2, lambda part_j: contributions(2 * sub * sub_pairs + part_j))
+                looped(2 * sub_pairs, 4, lambda part_j: contributions(2 * sub * sub_pairs + part_j))
 
         @pl.when(i > 0)
         def _():
@@ -729,7 +729,7 @@
             whole((own_blocks, gates)),
             whole((steps, rows, width)),
         ),
-        compiler_params=pltpu.CompilerParams(vmem_limit_bytes=32 * 2**20),
+        compiler_params=pltpu.CompilerParams(vmem_limit_bytes=62 * 2**20),
         name="grad_weights",
     )(lay, inputs_t, grad_pre, hidden)
     return (

time: 234 us -> 226 us (0.966)
  local copies, waits for them, and re-layouts: 6.75 us -> 2.4 us
  Pallas kernels: 223 us -> 220 us
    pallas_call x1, Pallas kernels: 214 us -> 208 us  [on_device(): pl.pallas_call(functools.partial(lstm_kernel, layers, units, groups), out...]
    unnamed x11 -> x3, local copies, waits for them, and re-layouts: 4.42 us -> 0.05 us
where the time goes in v5:
time: 226 us
  Pallas kernels  220 us (97%)
  other arithmetic  2.98 us (1%)
  local copies, waits for them, and re-layouts  2.4 us (1%)
    pallas_call x1, Pallas kernels, on_device(): pl.pallas_call(functools.partial(lstm_kernel, layers, units, groups), out...  208 us
    pallas_call x1, Pallas kernels, on_device(): pl.pallas_call(weight_kernel, grid=(own_blocks // 2,), out_shape=(jax.Sha...  11.5 us

profile of v5, /device:TPU:0, one launch (start us, length us, event | category | flops | bytes accessed | tf_op | source)
XLA Modules:
  0.0 226.1 jit_solution(17998986315158543505)
XLA Ops:
  0.6 0.0 copy-start
  0.6 0.8 eq.54
  1.5 0.8 reshape_squeeze.6
  2.2 0.2 fusion.1
  2.5 0.2 convert_reduce_fusion.1
  2.7 0.2 select_reduce_fusion
  2.9 0.1 slice_compare_fusion
  3.0 0.7 pad_convert_fusion.same_ref
  3.7 0.6 broadcast_add_fusion.perm_ref
  4.3 0.2 convert_reduce_fusion
  4.6 0.7 select_add_fusion.last_ref
  5.2 0.0 copy-done
  5.2 0.3 fusion
  5.6 0.7 copy.13
  6.3 208.3 %lstm.1 = (bf16[4,32,1024]{2,1,0:T(8,128)(2,1)}, bf16[256,64,128]{2,1,0:T(8,128)(2,1)}, bf16[16,128,256]{2,1,0:T(8,128)(2,1)}) custom-call(s32[16,32]{1,0:T(8,128)} %bitcast.19, s32[4,128]{1,0:T(4,128)} %broadcast_add_fusion.perm_ref, f32[4,128]{1,0:T(4,128)} %pad_convert_fusion.same_ref, s32[4,256]{1,0:T(4,128)} %select_add_fusion.last_ref, ...), custom_call_target="tpu_custom_call" | custom-call | tf_op jit(solution)/shard_map/lstm/pallas_call | solution.py:662
  214.6 11.5 %grad_weights.1 = (bf16[16,2048,256]{2,1,0:T(8,128)(2,1)}, f32[16,256]{1,0:T(8,128)}, bf16[4,32,1024]{2,1,0:T(8,128)(2,1)}) custom-call(s32[16,32]{1,0:T(8,128)} %bitcast.20, bf16[256,64,128]{2,1,0:T(8,128)(2,1)} %get-tuple-element.9.xt_ref, bf16[16,128,256]{2,1,0:T(8,128)(2,1)} %get-tuple-element.10.gp_ref, bf16[4,32,1024]{2,1,0:T(8,128)(2,1)} %get-tuple-element.11.hid_ref), custom_call_target="tpu_custom_call" | custom-call | tf_op jit(solution)/shard_map/grad_weights/pallas_call | solution.py:713
  (4 shorter events, 0.1 us)
Async XLA Ops:
  0.6 4.6 %copy-start = (bf16[256,1024]{1,0:T(8,128)(2,1)S(1)}, bf16[256,1024]{1,0:T(8,128)(2,1)}, u32[]{:S(2)}) copy-start(bf16[256,1024]{1,0:T(8,128)(2,1)} %param.7) | copy-start | bytes 1572868
